TPU v7x, 512 devices: a whole 4x8x8 slice. The times are simulated.
512 devices in a mesh: dp: 8 (over x, core), seq: 64 (over y, z).
Axes of the slice: x: 4, y: 8, z: 8, core: 2. Of those that a mesh axis runs over, the one named last changes fastest.
Arguments:
- hidden: bfloat16 [8, 8192, 2048], P('dp', 'seq'), may hold values from -7 to 7
- cotangent: bfloat16 [8, 8192, 2048], P('dp', 'seq'), may hold values from -6 to 6
- picks: int32 [8, 8192], P('dp', 'seq'), may hold values from 0 to 1, as said below
- gain: float32 [2048], replicated, may hold values from 0.5 to 1.5
- router: float32 [2048], replicated, may hold values from -0.125 to 0.125
- w_query: bfloat16 [2048, 1024], P('seq'), may hold values from -2 to 2
- w_kv: bfloat16 [2048, 256], P('seq'), may hold values from -2 to 2
- w_out: bfloat16 [1024, 2048], P('seq'), may hold values from -0.1875 to 0.1875
Outputs:
- mixed: bfloat16 [8, 8192, 2048], P('dp', 'seq')
- input_grad: bfloat16 [8, 8192, 2048], P('dp', 'seq')
- kv_grad: float32 [2048, 256], P('seq')
- router_grad: float32 [2048], P('seq')
Inputs may be any that keep to these rules, and one draw needn't show every extreme that they name: `picks`: every sequence has exactly 1024 picked tokens; each aligned block of 128 tokens has 0 to 32 of them, and in every sequence some block has exactly 32.
All inputs are finite; a program needn't handle non-finite values.
Results may differ from a plain program's by a relative error of at most 0.013.
The roundings to bfloat16 on the way count: a program that leaves them out, or rounds other values in their place, can miss the bound.
Values may be sent and summed in bfloat16 or wider, within the bound.
A program may use at most 64 MiB of HBM per device.

v0:
```python
import jax
import jax.numpy as jnp
from jax import lax
from jax.sharding import PartitionSpec as P

MODEL_WIDTH = 2048
QUERY_HEADS = 16
KEY_VALUE_HEADS = 2
HEAD_SIZE = 64


EPSILON = 1e-05


def carried_in(value, axis, combine, identity):
    peers, index = (lax.axis_size(axis), lax.axis_index(axis))
    everything = lax.all_gather(value, axis)
    start = jnp.broadcast_to(jnp.asarray(identity, value.dtype), value.shape)

    def lap(k, before):
        reached = k < index
        new = combine(before, everything[k])
        return jnp.where(reached, new, before)

    return lax.fori_loop(0, peers, lap, start)


def dot_transposed(left, right):
    return lax.dot_general(
        left, right, (((1,), (1,)), ((), ())), preferred_element_type=jnp.float32
    )


def weight_term(normed, grad_kv):
    return lax.dot_general(
        normed, grad_kv, (((0,), (0,)), ((), ())), preferred_element_type=jnp.float32
    )


def route_table(pick_mask, offset, devices_seq, slot_rows):
    token_count = pick_mask.shape[0]
    local_rank = jnp.cumsum(pick_mask) - pick_mask
    global_rank = offset + local_rank
    placed_at = global_rank % devices_seq * slot_rows + local_rank // devices_seq
    target = jnp.where(pick_mask > 0, placed_at, -1)
    route_hits = (
        lax.broadcasted_iota(jnp.int32, (devices_seq * slot_rows, token_count), 0)
        == target[None, :]
    )
    sent_rank = jnp.max(jnp.where(route_hits, global_rank[None, :], -1), axis=1)
    return (route_hits.astype(jnp.bfloat16), sent_rank.reshape(devices_seq, slot_rows))


def compact_table(got_rank, devices_seq, capacity_rows):
    rank_list = got_rank.reshape(-1)
    local_index = jnp.where(rank_list >= 0, rank_list // devices_seq, -1)
    matches = (
        lax.broadcasted_iota(jnp.int32, (capacity_rows, rank_list.shape[0]), 0)
        == local_index[None, :]
    )
    return matches.astype(jnp.bfloat16)


def select_rows(table, source):
    return jnp.dot(table, source, preferred_element_type=jnp.float32).astype(jnp.bfloat16)


def spread_rows(table, source):
    placed = lax.dot_general(
        table, source, (((0,), (0,)), ((), ())), preferred_element_type=jnp.float32
    )
    return placed.astype(jnp.bfloat16)


def local(hidden, cotangent, picks, gain, router, w_query, w_kv, w_out):
    devices_seq = lax.axis_size("seq")
    my_index = lax.axis_index("seq")
    token_count = hidden.shape[1]
    capacity_rows = token_count // 8
    slot_rows = (2 * capacity_rows + devices_seq - 1) // devices_seq
    key_value_width = KEY_VALUE_HEADS * HEAD_SIZE
    query_group_size = QUERY_HEADS // KEY_VALUE_HEADS
    head_scale = HEAD_SIZE ** (-0.5)
    token_half = hidden[0]
    token_rows = token_half.astype(jnp.float32)
    grad_rows = cotangent[0].astype(jnp.float32)
    pick_mask = picks[0]
    whole_query, whole_kv, whole_out = (
        lax.all_gather(w_query, "seq", axis=0, tiled=True),
        lax.all_gather(w_kv, "seq", axis=0, tiled=True),
        lax.all_gather(w_out, "seq", axis=0, tiled=True),
    )
    gate_prob = jax.nn.sigmoid(jnp.dot(token_rows, router, precision=lax.Precision.HIGHEST))
    offset = carried_in(
        jnp.sum(pick_mask), "seq", lambda earlier, later: earlier + later, jnp.int32(0)
    )
    route, sent_rank = route_table(pick_mask, offset, devices_seq, slot_rows)
    send_tokens = select_rows(route, token_half).reshape(devices_seq, slot_rows, MODEL_WIDTH)
    scaled_grad = (gate_prob[:, None] * grad_rows).astype(jnp.bfloat16)
    got_tokens, got_rank = (
        lax.all_to_all(send_tokens, "seq", split_axis=0, concat_axis=0, tiled=True),
        lax.all_to_all(sent_rank, "seq", split_axis=0, concat_axis=0, tiled=True),
    )
    compact = compact_table(got_rank, devices_seq, capacity_rows)
    block_float = select_rows(
        compact, got_tokens.reshape(devices_seq * slot_rows, MODEL_WIDTH)
    ).astype(jnp.float32)
    inv_norm = lax.rsqrt(jnp.mean(block_float * block_float, axis=1, keepdims=True) + EPSILON)
    normed = (block_float * inv_norm * gain[None, :]).astype(jnp.bfloat16)
    query_head_rows = jnp.dot(normed, whole_query, preferred_element_type=jnp.float32).astype(
        jnp.bfloat16
    )
    own_kv = jnp.dot(normed, whole_kv, preferred_element_type=jnp.float32).astype(jnp.bfloat16)
    every_key_value = lax.all_gather(own_kv, "seq", axis=0, tiled=True)
    key_total_count = every_key_value.shape[0]
    key_head_rows = every_key_value[:, :key_value_width].reshape(
        key_total_count, KEY_VALUE_HEADS, HEAD_SIZE
    )
    value_head_rows = every_key_value[:, key_value_width:].reshape(
        key_total_count, KEY_VALUE_HEADS, HEAD_SIZE
    )
    query_split_parts = query_head_rows.reshape(
        capacity_rows, KEY_VALUE_HEADS, query_group_size, HEAD_SIZE
    )
    position = lax.broadcasted_iota(jnp.int32, (key_total_count,), 0)
    key_rank = position // capacity_rows + devices_seq * (position % capacity_rows)
    query_rank = my_index + devices_seq * lax.broadcasted_iota(jnp.int32, (capacity_rows,), 0)
    allowed = (key_rank[None, :] <= query_rank[:, None])[:, None, None, :]
    scores = (
        jnp.einsum(
            "cgrd,ngd->cgrn", query_split_parts, key_head_rows, preferred_element_type=jnp.float32
        )
        * head_scale
    )
    scores = jnp.where(allowed, scores, -jnp.inf)
    score_top = jnp.max(scores, axis=3, keepdims=True)
    score_exp = jnp.exp(scores - score_top)
    attn_probs = score_exp / jnp.sum(score_exp, axis=3, keepdims=True)
    probs_half = attn_probs.astype(jnp.bfloat16)
    mixed_heads = jnp.einsum(
        "cgrn,ngd->cgrd", probs_half, value_head_rows, preferred_element_type=jnp.float32
    )
    mixed_heads = mixed_heads.astype(jnp.bfloat16).reshape(capacity_rows, QUERY_HEADS * HEAD_SIZE)
    block_out = jnp.dot(mixed_heads, whole_out, preferred_element_type=jnp.float32).astype(
        jnp.bfloat16
    )
    returned = lax.all_to_all(
        spread_rows(compact, block_out).reshape(devices_seq, slot_rows, MODEL_WIDTH),
        "seq",
        split_axis=0,
        concat_axis=0,
        tiled=True,
    )
    send_grads = select_rows(route, scaled_grad).reshape(devices_seq, slot_rows, MODEL_WIDTH)
    got_grads = lax.all_to_all(send_grads, "seq", split_axis=0, concat_axis=0, tiled=True)
    block_grad = select_rows(compact, got_grads.reshape(devices_seq * slot_rows, MODEL_WIDTH))
    gradient_heads = dot_transposed(block_grad, whole_out).astype(jnp.bfloat16)
    gradient_split = gradient_heads.reshape(
        capacity_rows, KEY_VALUE_HEADS, query_group_size, HEAD_SIZE
    )
    grad_probs = jnp.einsum(
        "cgrd,ngd->cgrn", gradient_split, value_head_rows, preferred_element_type=jnp.float32
    )
    inner_sum = jnp.sum(attn_probs * grad_probs, axis=3, keepdims=True)
    grad_scores = (attn_probs * (grad_probs - inner_sum)).astype(jnp.bfloat16)
    grad_query = (
        jnp.einsum("cgrn,ngd->cgrd", grad_scores, key_head_rows, preferred_element_type=jnp.float32)
        * head_scale
    )
    grad_query = grad_query.astype(jnp.bfloat16).reshape(capacity_rows, QUERY_HEADS * HEAD_SIZE)
    grad_keys = (
        jnp.einsum(
            "cgrn,cgrd->ngd", grad_scores, query_split_parts, preferred_element_type=jnp.float32
        )
        * head_scale
    )
    grad_values = jnp.einsum(
        "cgrn,cgrd->ngd", probs_half, gradient_split, preferred_element_type=jnp.float32
    )
    grad_terms = jnp.concatenate(
        [
            grad_keys.reshape(key_total_count, key_value_width),
            grad_values.reshape(key_total_count, key_value_width),
        ],
        axis=1,
    )
    grad_kv = lax.psum_scatter(grad_terms, "seq", scatter_dimension=0, tiled=True).astype(
        jnp.bfloat16
    )
    grad_normed = dot_transposed(grad_query, whole_query) + dot_transposed(grad_kv, whole_kv)
    upstream = grad_normed * gain[None, :]
    grad_block = inv_norm * upstream - block_float * inv_norm**3 * jnp.mean(
        upstream * block_float, axis=1, keepdims=True
    )
    grad_block = grad_block.astype(jnp.bfloat16)
    returned_grads = lax.all_to_all(
        spread_rows(compact, grad_block).reshape(devices_seq, slot_rows, MODEL_WIDTH),
        "seq",
        split_axis=0,
        concat_axis=0,
        tiled=True,
    )
    out_tokens = spread_rows(route, returned.reshape(devices_seq * slot_rows, MODEL_WIDTH)).astype(
        jnp.float32
    )
    mixed = (token_rows + gate_prob[:, None] * out_tokens).astype(jnp.bfloat16)
    through = jnp.sum(grad_rows * out_tokens, axis=1)
    grad_logit = through * gate_prob * (1.0 - gate_prob)
    router_part = jnp.dot(grad_logit, token_rows, precision=lax.Precision.HIGHEST)
    grad_tokens = spread_rows(
        route, returned_grads.reshape(devices_seq * slot_rows, MODEL_WIDTH)
    ).astype(jnp.float32)
    input_grad = (grad_rows + grad_logit[:, None] * router[None, :] + grad_tokens).astype(
        jnp.bfloat16
    )
    kv_part = weight_term(normed, grad_kv)
    kv_piece, router_piece = (
        lax.psum_scatter(kv_part, "seq", scatter_dimension=0, tiled=True),
        lax.psum_scatter(router_part, "seq", scatter_dimension=0, tiled=True),
    )
    kv_grad, router_grad = (
        lax.psum(kv_piece.astype(jnp.bfloat16), "dp").astype(jnp.float32),
        lax.psum(router_piece.astype(jnp.bfloat16), "dp").astype(jnp.float32),
    )
    return (mixed[None], input_grad[None], kv_grad, router_grad)


def solution(mesh):
    return jax.shard_map(
        local,
        mesh=mesh,
        in_specs=(
            P("dp", "seq", None),
            P("dp", "seq", None),
            P("dp", "seq"),
            P(),
            P(),
            P("seq", None),
            P("seq", None),
            P("seq", None),
        ),
        out_specs=(P("dp", "seq", None), P("dp", "seq", None), P("seq", None), P("seq")),
        check_vma=False,
    )
```

profile of v0, /device:TPU:1, one launch (start us, length us, event | category | flops | bytes accessed | tf_op | source)
XLA Modules:
  0.0 803.6 jit_solution(4762557109887954993)
XLA Ops:
  7.2 0.7 all-gather.4.cloned.1.call-update
  8.0 0.7 all-gather.8.cloned.1.call-update
  8.7 0.7 all-gather.6.cloned.1.call-update
  9.4 1.3 reduce_sum.54
  10.7 1.0 reduce-window_clone.1
  11.7 1.4 fusion.88
  13.0 1.4 dynamic-update-slice
  14.4 26.6 %all-reduce = s32[64]{0:T(128)S(1)} all-reduce(s32[64]{0:T(128)S(1)} %dynamic-update-slice), channel_id=1, replica_groups=mesh['dp'=8,'seq'=64] {'seq'}, use_global_device_ids=true, to_apply=%add | all-reduce | flops 64 | bytes 512
  41.0 81.0 %while.13 = (s32[]{:T(128)}, s32[]{:T(128)}, s32[]{:T(128)}, s32[64]{0:T(128)S(1)}, s32[]{:T(128)}) while((s32[]{:T(128)}, s32[]{:T(128)}, s32[]{:T(128)}, s32[64]{0:T(128)S(1)}, s32[]{:T(128)}) %tuple.42), condition=%wide.region_2.3_spmd, body=%wide.region_1.2_spmd.sunk | while | flops 5 | bytes 115 | solution.py:25
  42.3 0.6 dynamic_slice.8
  43.5 0.6 dynamic_slice.8
  46.1 0.6 dynamic_slice.8
  47.3 0.6 dynamic_slice.8
  48.6 0.6 dynamic_slice.8
  49.9 0.6 dynamic_slice.8
  52.4 0.6 dynamic_slice.8
  53.7 0.6 dynamic_slice.8
  54.9 0.6 dynamic_slice.8
  56.2 0.6 dynamic_slice.8
  58.7 0.6 dynamic_slice.8
  60.0 0.6 dynamic_slice.8
  61.3 0.6 dynamic_slice.8
  63.8 0.6 dynamic_slice.8
  122.0 0.7 add_bitcast_fusion
  122.8 0.7 copy.54
  123.5 5.9 all-to-all-start
  129.4 1.6 fusion.25
  131.0 1.3 fusion.8
  132.9 0.8 reduce.3
  133.7 0.9 reshape.220
  134.5 5.7 all-to-all-done
  140.2 6.5 all-to-all-start.3
  146.7 1.3 fusion.6
  148.0 0.8 reduce.2
  148.7 0.9 reshape.216
  149.6 9.6 %all-to-all-done.3 = bf16[64,2,1024]{2,1,0:T(2,128)(2,1)S(1)} async-done(((bf16[64,2,1024]{2,1,0:T(2,128)(2,1)}), bf16[64,2,1024]{2,1,0:T(2,128)(2,1)S(1)}, u32[]{:S(2)}, u32[]{:S(2)}) %all-to-all-start.3) | async-done | bytes 262176 | tf_op jit(solution)/shard_map/all_to_all | solution.py:155
  159.2 4.6 all-to-all-start.1
  164.0 1.2 reduce.1
  165.5 11.7 %all-to-all-done.1 = bf16[64,2,1024]{2,1,0:T(2,128)(2,1)S(1)} async-done(((bf16[64,2,1024]{2,1,0:T(2,128)(2,1)}), bf16[64,2,1024]{2,1,0:T(2,128)(2,1)S(1)}, u32[]{:S(2)}, u32[]{:S(2)}) %all-to-all-start.1) | async-done | bytes 262176 | tf_op jit(solution)/shard_map/all_to_all | solution.py:101
  177.9 1.5 convolution_convert_fusion.11
  179.4 37.7 %all_gather.21 = bf16[1024,256]{1,0:T(8,128)(2,1)S(1)} all-gather(bf16[16,256]{1,0:T(8,128)(2,1)S(1)} %convolution_convert_fusion.11), channel_id=1, replica_groups=mesh['dp'=8,'seq'=64] {'seq'}, dimensions={0}, use_global_device_ids=true | all-gather | bytes 532480 | tf_op jit(solution)/shard_map/all_gather | solution.py:114
  217.5 3.5 fusion.21
  221.1 54.0 %all-gather.6.cloned.1.call-done = bf16[2048,1024]{1,0:T(8,128)(2,1)} async-done(((bf16[32,1024]{1,0:T(8,128)(2,1)}), bf16[2048,1024]{1,0:T(8,128)(2,1)}) %all-gather.6.cloned.1.call-update) | async-done | bytes 4194320 | tf_op jit(solution)/shard_map/all_gather | solution.py:89
  275.1 2.8 convolution_convert_fusion.10
  280.2 1.4 copy.69
  281.9 239.5 %reduce-scatter.7.cloned.1.call-done = f32[16,256]{1,0:T(8,128)} async-done(((f32[1024,256]{1,0:T(8,128)}), f32[16,256]{1,0:T(8,128)}) %reduce-scatter.7.cloned.1.call-update) | async-done | bytes 16400
  521.4 0.8 copy.70
  522.2 1.9 fusion.95
  525.2 3.0 fusion.7
  528.2 0.9 reduce.4
  529.1 0.9 reshape.218
  529.9 8.7 %all-to-all-start.2 = ((bf16[64,2,1024]{2,1,0:T(2,128)(2,1)}), bf16[64,2,1024]{2,1,0:T(2,128)(2,1)S(1)}, u32[]{:S(2)}, u32[]{:S(2)}) async-start(bf16[64,2,1024]{2,1,0:T(2,128)(2,1)} %reshape.218), calls=%async_computation.2 | async-start | bytes 524288 | tf_op jit(solution)/shard_map/all_to_all | solution.py:147
  539.1 3.5 fusion.94
  542.6 8.6 %all-to-all-done.2 = bf16[64,2,1024]{2,1,0:T(2,128)(2,1)S(1)} async-done(((bf16[64,2,1024]{2,1,0:T(2,128)(2,1)}), bf16[64,2,1024]{2,1,0:T(2,128)(2,1)S(1)}, u32[]{:S(2)}, u32[]{:S(2)}) %all-to-all-start.2) | async-done | bytes 262176 | tf_op jit(solution)/shard_map/all_to_all | solution.py:147
  552.2 0.8 reduce.5
  553.0 0.9 reshape.222
  553.9 4.6 all-to-all-start.4
  558.5 1.3 fusion.26
  560.1 118.4 %all-reduce.1 = bf16[2048]{0:T(1024)(128)(2,1)S(1)} all-reduce(f32[2048]{0:T(1024)S(1)} %bitcast.143), channel_id=4, replica_groups=mesh['dp'=8,'seq'=64] {'seq'}, use_global_device_ids=true, to_apply=%region_14.15.clone | all-reduce | flops 2048 | bytes 12288
  678.9 1.2 fusion.5
  680.0 89.7 %reduce-scatter.5.cloned.1.call-done = f32[32,256]{1,0:T(8,128)} async-done(((f32[2048,256]{1,0:T(8,128)}), f32[32,256]{1,0:T(8,128)}) %reduce-scatter.5.cloned.1.call-update) | async-done | bytes 32784 | tf_op jit(solution)/shard_map/reduce_scatter | solution.py:218
  769.7 0.8 convert_element_type.134
  770.5 25.5 %all-reduce.2 = (bf16[32,256]{1,0:T(8,128)(2,1)S(1)}, bf16[32]{0:T(256)(128)(2,1)S(1)}) all-reduce(bf16[32,256]{1,0:T(8,128)(2,1)S(1)} %convert_element_type.134, bf16[32]{0:T(256)(128)(2,1)S(1)} %dynamic-slice.4), channel_id=1, replica_groups=mesh['dp'=8,'seq'=64] {'dp'}, use_global_device_ids=true, to_apply=%region_13.14 | all-reduce | flops 8224 | bytes 32896 | tf_op jit(solution)/shard_map/psum | solution.py:222
  796.5 0.6 convert_element_type.135
  (108 shorter events, 37.1 us)
Async XLA Ops:
  7.2 170.6 %copy-start.4 = (f32[2048]{0:T(1024)S(1)}, f32[2048]{0:T(1024)}, u32[]{:S(2)}) copy-start(f32[2048]{0:T(1024)} %param.13) | copy-start | bytes 24580
  7.2 170.7 %all-gather.4.cloned.1.call-start = ((), (), s32[]{:S(2)}) async-start(), calls=%async_computation.7 | async-start | bytes 1064960 | tf_op jit(solution)/shard_map/all_gather | solution.py:90
  7.9 209.6 %all-gather.8.cloned.1.call-start = ((), (), s32[]{:S(2)}) async-start(), calls=%async_computation.9 | async-start | bytes 4259840 | tf_op jit(solution)/shard_map/all_gather | solution.py:91
  8.7 266.4 %all-gather.6.cloned.1.call-start = ((), (), s32[]{:S(2)}) async-start(), calls=%async_computation.8 | async-start | bytes 4259840 | tf_op jit(solution)/shard_map/all_gather | solution.py:89
  123.5 16.7 %all-to-all-start = ((s32[64,1,1]{2,1,0:T(1,128)}), s32[64,1,1]{2,1,0:T(1,128)S(1)}, u32[]{:S(2)}, u32[]{:S(2)}) async-start(s32[64,1,1]{2,1,0:T(1,128)} %copy.54), calls=%async_computation | async-start | bytes 65536 | tf_op jit(solution)/shard_map/all_to_all | solution.py:102
  140.2 19.0 %all-to-all-start.3 = ((bf16[64,2,1024]{2,1,0:T(2,128)(2,1)}), bf16[64,2,1024]{2,1,0:T(2,128)(2,1)S(1)}, u32[]{:S(2)}, u32[]{:S(2)}) async-start(bf16[64,2,1024]{2,1,0:T(2,128)(2,1)} %reshape.220), calls=%async_computation.3 | async-start | bytes 524288 | tf_op jit(solution)/shard_map/all_to_all | solution.py:155
  159.2 18.0 %all-to-all-start.1 = ((bf16[64,2,1024]{2,1,0:T(2,128)(2,1)}), bf16[64,2,1024]{2,1,0:T(2,128)(2,1)S(1)}, u32[]{:S(2)}, u32[]{:S(2)}) async-start(bf16[64,2,1024]{2,1,0:T(2,128)(2,1)} %reshape.216), calls=%async_computation.1 | async-start | bytes 524288 | tf_op jit(solution)/shard_map/all_to_all | solution.py:101
  163.9 357.5 %reduce-scatter.7.cloned.1.call-start = ((), (), s32[]{:S(2)}) async-start(), calls=%async_computation.11 | async-start | bytes 1064960
  281.7 488.1 %reduce-scatter.5.cloned.1.call-start = ((), (), s32[]{:S(2)}) async-start(), calls=%async_computation.10 | async-start | bytes 2129920 | tf_op jit(solution)/shard_map/reduce_scatter | solution.py:218
  528.2 23.2 %copy-start.2 = (bf16[2048,256]{1,0:T(8,128)(2,1)S(1)}, bf16[2048,256]{1,0:T(8,128)(2,1)}, u32[]{:S(2)}) copy-start(bf16[2048,256]{1,0:T(8,128)(2,1)} %all-gather.4.cloned.1.call-done) | copy-start | bytes 3145732
  529.9 21.2 %all-to-all-start.2 = ((bf16[64,2,1024]{2,1,0:T(2,128)(2,1)}), bf16[64,2,1024]{2,1,0:T(2,128)(2,1)S(1)}, u32[]{:S(2)}, u32[]{:S(2)}) async-start(bf16[64,2,1024]{2,1,0:T(2,128)(2,1)} %reshape.218), calls=%async_computation.2 | async-start | bytes 524288 | tf_op jit(solution)/shard_map/all_to_all | solution.py:147
  539.1 19.4 %copy-start = (bf16[1,128,2048]{2,1,0:T(8,128)(2,1)S(1)}, bf16[1,128,2048]{2,1,0:T(8,128)(2,1)}, u32[]{:S(2)}) copy-start(bf16[1,128,2048]{2,1,0:T(8,128)(2,1)} %param.10) | copy-start | bytes 1572868
  539.1 19.4 %copy-start.1 = (bf16[1,128,2048]{2,1,0:T(8,128)(2,1)S(1)}, bf16[1,128,2048]{2,1,0:T(8,128)(2,1)}, u32[]{:S(2)}) copy-start(bf16[1,128,2048]{2,1,0:T(8,128)(2,1)} %param.11) | copy-start | bytes 1572868
  542.6 136.3 %copy-start.3 = (f32[2048]{0:T(1024)S(1)}, f32[2048]{0:T(1024)}, u32[]{:S(2)}) copy-start(f32[2048]{0:T(1024)} %param.14) | copy-start | bytes 24580
  553.9 124.8 %all-to-all-start.4 = ((bf16[64,2,1024]{2,1,0:T(2,128)(2,1)}), bf16[64,2,1024]{2,1,0:T(2,128)(2,1)S(1)}, u32[]{:S(2)}, u32[]{:S(2)}) async-start(bf16[64,2,1024]{2,1,0:T(2,128)(2,1)} %reshape.222), calls=%async_computation.4 | async-start | bytes 524288 | tf_op jit(solution)/shard_map/all_to_all | solution.py:196
Sparse Core Ops, SparseCore 0:
  11.0 83.4 all-gather.3
  97.5 91.8 all-gather.7
  192.4 82.6 all-gather.5
  281.8 239.5 reduce-scatter.6
  525.9 243.8 reduce-scatter.4
where the time goes:
time: 808 us; the launch traced here: 804 us
  waiting for transfers between devices  421 us (52%)
  blocking collectives  208 us (26%)
  local copies, waits for them, and re-layouts  49.1 us (6%)
  loops' own time  43.5 us (5%)
  starting transfers between devices  30.7 us (4%)
  matrix products  26.7 us (3%)
  between operations  14.8 us (2%)
  other arithmetic  9.89 us (1%)
    unnamed x6, waiting for transfers between devices  242 us
    unnamed x2, blocking collectives  145 us
    reduce_scatter x1, waiting for transfers between devices, local(): lax.psum_scatter(kv_part, 'seq', scatter_dimension=0, tiled=True)  89.7 us
    all_gather x1, waiting for transfers between devices, local(): lax.all_gather(w_query, 'seq', axis=0, tiled=True)  54 us
    another operation x1, loops' own time, carried_in(): return lax.fori_loop(0, peers, lap, start)  43.5 us
    all_gather x1, blocking collectives, local(): every_key_value = lax.all_gather(own_kv, 'seq', axis=0, tiled=True)  37.7 us
    dynamic_slice x64, local copies, waits for them, and re-layouts, lap(): new = combine(before, everything[k])  37.5 us
    psum x1, blocking collectives, local(): lax.psum(kv_piece.astype(jnp.bfloat16), 'dp').astype(jnp.float32)  25.5 us
  transfers between devices with their start and end apart: 10, of which 7 were waited for; matrix products, arithmetic and copies ran while one was open for 9% of the time, Pallas kernels for 0%

commit v1 on v0

v1 whole, which is shorter than its diff:
```python
import functools
import math

import jax
import jax.numpy as jnp
from jax import lax
from jax.experimental import pallas as pl
from jax.experimental.pallas import tpu as pltpu
from jax.sharding import PartitionSpec as P

MESH = pl.DeviceIdType.MESH
EPSILON = 1e-05
SLOTS = 32
HEAD = 64
F32, BF16 = jnp.float32, jnp.bfloat16
KEY_MARK = 2.0**100
KEY_BOUND = 2.0**64
NEGATIVE = -1e30
FAR = 1 << 30
WIRE = BF16


def dot(left, right, left_dim=1, right_dim=0):
    return lax.dot_general(
        left, right, (((left_dim,), (right_dim,)), ((), ())), preferred_element_type=F32
    )


def copy_to(source, target, send_sem, recv_sem, device):
    return pltpu.make_async_remote_copy(
        src_ref=source,
        dst_ref=target,
        send_sem=send_sem,
        recv_sem=recv_sem,
        device_id=device,
        device_id_type=MESH,
    )


def kernel(
    n, n_dp, width, group_heads,
    hid, cot, picks, gain, router, wq, wkv, wo,
    mixed_out, igrad_out, kvgrad_out, rgrad_out,
    wproj, wout, kv, kvt, scores, dprobs, qpad, opad, dkv, got_dkv, part, got_part,
    gkv, normed, normed_t, share, got_share, total, row_a, row_b, row_d,
    block, block_grad, block_out, dqkv, upstream,
    p1_send, p1_recv, ring_send, ring_recv, sib_send, sib_recv,
    a_send, a_recv, b_send, b_recv, d_send, d_recv,
):
    seq, dp = lax.axis_index("seq"), lax.axis_index("dp")
    core = lax.rem(dp, 2)
    y, z = lax.div(seq, n), lax.rem(seq, n)
    a = z + core * (y - z)
    b = y + core * (z - y)
    keys = n * SLOTS
    half_heads = group_heads * HEAD
    lanes = 2 * group_heads * SLOTS
    half_width = width // 2
    chunk = keys

    def seq_of(b_, a_):
        return (1 - core) * (b_ * n + a_) + core * (a_ * n + b_)

    def peer_a(j):
        return (dp, seq_of(b, lax.rem(a + j, n)))

    def peer_b(j):
        return (dp, seq_of(lax.rem(b + j, n), a))

    def peer_d(j):
        return (lax.rem(dp + j, n_dp), seq)

    sibling = (dp + 1 - 2 * core, seq)

    def each(count, body):
        def step(j, carry):
            body(j)
            return carry

        lax.fori_loop(0, count, step, 0)

    def others(count, body):
        def step(j, carry):
            body(j)
            return carry

        lax.fori_loop(1, count, step, 0)

    barrier = pltpu.get_barrier_semaphore()

    def greet(device):
        pl.semaphore_signal(barrier, inc=1, device_id=device, device_id_type=MESH)

    others(n, lambda j: greet(peer_a(j)))
    others(n, lambda j: greet(peer_b(j)))
    others(n_dp, lambda j: greet(peer_d(j)))

    for side in (0, 1):

        @pl.when(core == side)
        def _():
            cols = slice(side * half_heads, (side + 1) * half_heads)
            wproj[side, y, z, :, :half_heads] = wq[:, cols]
            wproj[side, y, z, :, half_heads:] = wkv[:, side * 128 : (side + 1) * 128]
            wout[side, y, z] = wo[:, side * half_width : (side + 1) * half_width]

    pl.semaphore_wait(barrier, 2 * (n - 1) + n_dp - 1)

    def first(which, ref):
        def make(j):
            own = ref.at[core, y, z]
            return copy_to(own, own, p1_send.at[which, j], p1_recv.at[which, j], peer_a(j))

        return make

    def along_a(which, source, target):
        def make(j):
            return copy_to(source(j), target, a_send.at[which, j], a_recv.at[which, j], peer_a(j))

        return make

    def along_b(which, source, target):
        def make(j):
            return copy_to(source(j), target, b_send.at[which, j], b_recv.at[which, j], peer_b(j))

        return make

    def along_d(which, ref):
        def make(j):
            return copy_to(
                ref.at[dp], ref.at[dp], d_send.at[which, j], d_recv.at[which, j], peer_d(j)
            )

        return make

    def start(make, count=n):
        others(count, lambda j: make(j).start())

    def arrived(make, count=n):
        others(count, lambda j: make(j).wait_recv())

    def sent(make, count=n):
        others(count, lambda j: make(j).wait_send())

    last = n // 2 - 1

    def slab(ref, side, k, part_of=None):
        rows = slice(None) if part_of is None else pl.ds(part_of * (n // 2), n // 2)
        return ref.at[0, k, rows] if side == 0 else ref.at[1, rows, k]

    def ring_start(which, ref, step):
        for side in (0, 1):

            @pl.when(core == side)
            def _():
                for way, block_id, device in (
                    (0, lax.rem(b + n - step, n), peer_b(1)),
                    (1, lax.rem(b + step, n), peer_b(n - 1)),
                ):
                    piece = slab(ref, side, block_id, way if step == last else None)
                    copy_to(
                        piece,
                        piece,
                        ring_send.at[which, step, way],
                        ring_recv.at[which, step, way],
                        device,
                    ).start()

    def ring_copy(which, ref, step, way):
        piece = slab(ref, 0, 0, way if step == last else None)
        return copy_to(
            piece,
            piece,
            ring_send.at[which, step, way],
            ring_recv.at[which, step, way],
            peer_b(1),
        )

    def ring_arrived(which, ref, step):
        for way in (0, 1):
            ring_copy(which, ref, step, way).wait_recv()

    def sib_start(which, ref, slot, block_id):
        for side in (0, 1):

            @pl.when(core == side)
            def _():
                piece = slab(ref, side, block_id)
                copy_to(
                    piece, piece, sib_send.at[which, slot], sib_recv.at[which, slot], sibling
                ).start()

    def sib_copy(which, ref, slot):
        piece = slab(ref, 0, 0)
        return copy_to(piece, piece, sib_send.at[which, slot], sib_recv.at[which, slot], sibling)

    def pass_on(which, ref, step):
        ring_arrived(which, ref, step)
        if step < last:
            ring_start(which, ref, step + 1)
        sib_start(which, ref, 1 + 2 * step, lax.rem(b + n - 1 - step, n))
        if step < last:
            sib_start(which, ref, 2 + 2 * step, lax.rem(b + 1 + step, n))

    start(first(0, wproj))
    start(first(1, wout))

    tokens = hid.shape[1]
    row_id = lax.broadcasted_iota(jnp.int32, (tokens, tokens), 0)
    col_id = lax.broadcasted_iota(jnp.int32, (tokens, tokens), 1)
    pick_row = picks[...].astype(F32)
    pick_wide = jnp.broadcast_to(pick_row, (tokens, tokens))
    pick_col = jnp.sum(jnp.where(row_id == col_id, pick_wide, 0.0), axis=1, keepdims=True)
    rank_col = jnp.sum(jnp.where(col_id < row_id, pick_wide, 0.0), axis=1, keepdims=True)
    pick_tall = jnp.broadcast_to(pick_col, (tokens, tokens))
    rank_row = jnp.sum(jnp.where(row_id < col_id, pick_tall, 0.0), axis=0, keepdims=True)
    slot_row = lax.broadcasted_iota(jnp.int32, (SLOTS, tokens), 0).astype(F32)
    slot_col = lax.broadcasted_iota(jnp.int32, (tokens, SLOTS), 1).astype(F32)
    pack = jnp.where((slot_row == rank_row) & (pick_row > 0.5), 1.0, 0.0)
    spread = jnp.where((slot_col == rank_col) & (pick_col > 0.5), 1.0, 0.0).astype(BF16)
    used = jnp.sum(pack, axis=1, keepdims=True)
    pack = pack.astype(BF16)

    n_chunks = width // chunk

    def at(i):
        return pl.ds(pl.multiple_of(i * chunk, chunk), chunk)

    def gate_step(i, acc):
        return acc + hid[0, :, at(i)].astype(F32) * router[:, at(i)]

    logit = lax.fori_loop(0, n_chunks, gate_step, jnp.zeros((tokens, chunk), F32))
    gate = jax.nn.sigmoid(jnp.sum(logit, axis=1, keepdims=True))

    def pack_step(i, acc):
        rows = dot(pack, hid[0, :, at(i)])
        block[:, at(i)] = rows
        scaled = (gate * cot[0, :, at(i)].astype(F32)).astype(BF16)
        block_grad[:, at(i)] = dot(pack, scaled).astype(BF16)
        return acc + rows * rows

    squares = lax.fori_loop(0, n_chunks, pack_step, jnp.zeros((SLOTS, chunk), F32))
    inv_norm = lax.rsqrt(jnp.sum(squares, axis=1, keepdims=True) * (1.0 / width) + EPSILON)

    def norm_step(i):
        normed[a, :, at(i)] = (block[:, at(i)] * inv_norm * gain[:, at(i)]).astype(BF16)

    each(n_chunks, norm_step)

    arrived(first(0, wproj))
    ring_start(0, wproj, 0)
    sib_start(0, wproj, 0, b)
    for step in range(last + 1):
        pass_on(0, wproj, step)
    arrived(first(1, wout))
    ring_start(1, wout, 0)
    sib_start(1, wout, 0, b)
    for slot in range(n):
        sib_copy(0, wproj, slot).wait_recv()

    def project(side):
        def step(i, acc):
            return acc + dot(normed[a, :, at(i)], wproj[side, i].reshape(chunk, -1))

        zero = jnp.zeros((SLOTS, half_heads + 128), F32)
        return lax.fori_loop(0, n_chunks, step, zero).astype(BF16)

    low_lane = lax.broadcasted_iota(jnp.int32, (SLOTS, 128), 1) < HEAD

    def pad_heads(ref, rows, group):
        for i in range(group_heads // 2):
            pair = rows[:, i * 128 : (i + 1) * 128]
            for parity in (0, 1):
                moved = pair if parity == group else pltpu.roll(pair, HEAD, 1)
                kept = jnp.where(low_lane, moved, 0.0) if group == 0 else jnp.where(low_lane, 0.0, moved)
                at_row = (group * group_heads + 2 * i + parity) * SLOTS
                ref[at_row : at_row + SLOTS, :] = kept.astype(BF16)

    def join_heads(both):
        tall = jnp.transpose(both)
        groups = []
        for group in (0, 1):
            pairs = []
            for i in range(group_heads // 2):
                at_row = (group * group_heads + 2 * i) * SLOTS
                even = tall[at_row : at_row + SLOTS, :]
                odd = tall[at_row + SLOTS : at_row + 2 * SLOTS, :]
                if group == 0:
                    pairs.append(jnp.where(low_lane, even, pltpu.roll(odd, HEAD, 1)))
                else:
                    pairs.append(jnp.where(low_lane, pltpu.roll(even, HEAD, 1), odd))
            groups.append(jnp.concatenate(pairs, axis=1))
        return groups

    low = project(0).astype(F32)
    high = project(1).astype(F32)
    lane_id = lax.broadcasted_iota(jnp.int32, (SLOTS, 128), 1)
    own_keys = jnp.where((lane_id == 0) & (used < 0.5), KEY_MARK, low[:, half_heads:])
    kv[b, a, :, :128] = own_keys.astype(BF16)
    kv[b, a, :, 128:] = high[:, half_heads:].astype(BF16)
    kv_first = along_a(0, lambda j: kv.at[b, a], kv.at[b, a])
    kv_second = along_b(0, lambda j: kv.at[b], kv.at[b])
    start(kv_first)
    pad_heads(qpad, low[:, :half_heads], 0)
    pad_heads(qpad, high[:, :half_heads], 1)
    pass_on(1, wout, 0)
    arrived(kv_first)
    start(kv_second)
    for step in range(1, last):
        pass_on(1, wout, step)
    arrived(kv_second)

    key_row = lax.broadcasted_iota(jnp.int32, (keys, 1), 0)
    query_at = seq * SLOTS + (lax.broadcasted_iota(jnp.int32, (1, lanes), 1) & (SLOTS - 1))
    scale = HEAD**-0.5

    def score_step(i, top):
        rows = kv[i].reshape(keys, 256).astype(F32)
        kvt[i] = jnp.transpose(rows).astype(BF16)
        key_at = seq_of(i, key_row >> 5) * SLOTS + (key_row & (SLOTS - 1))
        key_at = jnp.where(rows[:, 0:1] < KEY_BOUND, key_at, FAR)
        s = dot(rows[:, :128].astype(BF16), qpad[...], 1, 1) * scale
        s = jnp.where(key_at <= query_at, s, NEGATIVE)
        scores[i] = s
        return jnp.maximum(top, jnp.max(s, axis=0, keepdims=True))

    top = lax.fori_loop(0, n, score_step, jnp.full((1, lanes), NEGATIVE, F32))

    def exp_step(i, acc):
        e = jnp.exp(scores[i] - top)
        scores[i] = e
        return acc + jnp.sum(e, axis=0, keepdims=True)

    inv_sum = 1.0 / lax.fori_loop(0, n, exp_step, jnp.zeros((1, lanes), F32))

    if last > 0:
        pass_on(1, wout, last)
    normed_gather = along_a(1, lambda j: normed.at[a], normed.at[a])
    start(normed_gather)
    for slot in range(n):
        sib_copy(1, wout, slot).wait_recv()

    out_rows = n * wout.shape[3]

    def out_at(i):
        return pl.ds(pl.multiple_of(i * out_rows, out_rows), out_rows)

    def head_grad_step(i):
        acc = jnp.zeros((SLOTS, out_rows), F32)
        for side in (0, 1):
            part_grad = block_grad[:, side * half_width : (side + 1) * half_width]
            acc += dot(part_grad, wout[side, i].reshape(out_rows, half_width), 1, 1)
        upstream[:, out_at(i)] = acc

    each(n, head_grad_step)
    for group in (0, 1):
        rows = upstream[:, group * half_heads : (group + 1) * half_heads]
        pad_heads(opad, rows, group)

    def prob_step(i, carry):
        inner, mixed_t = carry
        p = scores[i] * inv_sum
        scores[i] = p
        dp_ = dot(kv[i].reshape(keys, 256)[:, 128:], opad[...], 1, 1)
        dprobs[i] = dp_
        mixed_t += dot(kvt[i, 128:, :], p.astype(BF16))
        return inner + jnp.sum(p * dp_, axis=0, keepdims=True), mixed_t

    inner, mixed_t = lax.fori_loop(
        0, n, prob_step, (jnp.zeros((1, lanes), F32), jnp.zeros((128, lanes), F32))
    )

    send_dkv = along_b(1, lambda j: dkv.at[lax.rem(b + j, n)], got_dkv.at[b])

    def grad_step(j, query_t):
        i = lax.rem(b + j, n)
        p = scores[i]
        ds = (p * (dprobs[i] - inner)).astype(BF16)
        dkv[i, :, :128] = (dot(ds, qpad[...]) * scale).astype(WIRE)
        dkv[i, :, 128:] = dot(p.astype(BF16), opad[...]).astype(WIRE)

        @pl.when(j < n)
        def _():
            send_dkv(lax.rem(j, n)).start()

        return query_t + dot(kvt[i, :128, :], ds)

    query_t = lax.fori_loop(1, n + 1, grad_step, jnp.zeros((128, lanes), F32))

    heads = jnp.concatenate(join_heads(mixed_t), axis=1).astype(BF16)
    for side in (0, 1):
        rows = wout[side].reshape(n * out_rows, half_width)
        block_out[:, side * half_width : (side + 1) * half_width] = dot(heads, rows).astype(BF16)

    def mix_step(i, acc):
        out_tokens = dot(spread, block_out[:, at(i)])
        mixed_out[0, :, at(i)] = (hid[0, :, at(i)].astype(F32) + gate * out_tokens).astype(BF16)
        return acc + cot[0, :, at(i)].astype(F32) * out_tokens

    through = lax.fori_loop(0, n_chunks, mix_step, jnp.zeros((tokens, chunk), F32))
    through = jnp.sum(through, axis=1, keepdims=True)
    grad_logit = through * gate * (1.0 - gate)

    def router_step(i):
        term = hid[0, :, at(i)].astype(F32) * grad_logit
        row_a[a, :, at(i)] = jnp.sum(term, axis=0, keepdims=True)

    each(n_chunks, router_step)
    router_first = along_a(2, lambda j: row_a.at[a], row_a.at[a])
    router_second = along_b(2, lambda j: row_b.at[b], row_b.at[b])
    router_third = along_d(0, row_d)
    start(router_first)

    for group, rows in enumerate(join_heads(query_t * scale)):
        dqkv[group, :, :half_heads] = rows.astype(BF16)
    arrived(normed_gather)

    def turn_step(i):
        rows = normed[:, :, at(i)].reshape(keys, chunk).astype(F32)
        normed_t[i] = jnp.transpose(rows).astype(BF16).reshape(n, SLOTS, keys)

    each(n_chunks, turn_step)

    arrived(send_dkv)
    mine = dkv[b].astype(F32)
    mine = lax.fori_loop(
        1, n, lambda j, acc: acc + got_dkv[lax.rem(b + j, n)].astype(F32), mine
    )
    part[...] = mine.reshape(n, SLOTS, 256)
    send_part = along_a(3, lambda j: part.at[lax.rem(a + j, n)], got_part.at[a])
    start(send_part)
    arrived(router_first)
    row_b[b] = jnp.sum(row_a[...], axis=0)
    start(router_second)
    arrived(send_part)
    own = part[a]
    own = lax.fori_loop(1, n, lambda j, acc: acc + got_part[lax.rem(a + j, n)], own)
    grad_kv = own.astype(BF16)
    gkv[a] = grad_kv
    gkv_gather = along_a(4, lambda j: gkv.at[a], gkv.at[a])
    start(gkv_gather)
    dqkv[0, :, half_heads:] = grad_kv[:, :128]
    dqkv[1, :, half_heads:] = grad_kv[:, 128:]

    def back_step(i, acc):
        grads = dot(dqkv[0], wproj[0, i].reshape(chunk, -1), 1, 1)
        grads += dot(dqkv[1], wproj[1, i].reshape(chunk, -1), 1, 1)
        u = grads * gain[:, at(i)]
        upstream[:, at(i)] = u
        return acc + u * block[:, at(i)]

    along = lax.fori_loop(0, n_chunks, back_step, jnp.zeros((SLOTS, chunk), F32))
    along = jnp.sum(along, axis=1, keepdims=True) * (1.0 / width)

    arrived(gkv_gather)
    every = gkv[...].reshape(keys, 256)

    def share_step(i):
        place = (1 - core) * (i * n + a) + core * (a * n + i)
        share[i] = dot(normed_t[lax.div(place, n), lax.rem(place, n)], every)

    each(n, share_step)
    send_share = along_b(3, lambda j: share.at[lax.rem(b + j, n)], got_share.at[b])
    start(send_share)

    arrived(router_second)
    row_d[dp] = jnp.sum(row_b[...], axis=0)
    start(router_third, n_dp)

    cubed = inv_norm * inv_norm * inv_norm * along

    def input_step(i):
        rows = inv_norm * upstream[:, at(i)] - block[:, at(i)] * cubed
        tokens_grad = dot(spread, rows.astype(BF16))
        grads = cot[0, :, at(i)].astype(F32) + grad_logit * router[:, at(i)] + tokens_grad
        igrad_out[0, :, at(i)] = grads.astype(BF16)

    each(n_chunks, input_step)

    arrived(send_share)
    own = share[b]
    own = lax.fori_loop(1, n, lambda j, acc: acc + got_share[lax.rem(b + j, n)], own)
    total[dp] = own
    send_total = along_d(1, total)
    start(send_total, n_dp)
    arrived(router_third, n_dp)
    row = jnp.sum(row_d[...], axis=0)
    per_tile = 128 // SLOTS
    tile = jnp.zeros((1, SLOTS), F32)
    for i in range(width // SLOTS):
        tile = jnp.where(seq == i, row[:, i * SLOTS : (i + 1) * SLOTS], tile)
    rgrad_out[...] = tile
    arrived(send_total, n_dp)
    kvgrad_out[...] = jnp.sum(total[...], axis=0)

    sent(first(0, wproj))
    sent(first(1, wout))
    for which, ref in ((0, wproj), (1, wout)):
        for step in range(last + 1):
            for way in (0, 1):
                ring_copy(which, ref, step, way).wait_send()
        for slot in range(n):
            sib_copy(which, ref, slot).wait_send()
    for make in (kv_first, kv_second, normed_gather, send_dkv, router_first, router_second):
        sent(make)
    for make in (send_part, gkv_gather, send_share):
        sent(make)
    sent(router_third, n_dp)
    sent(send_total, n_dp)


def local(hidden, cotangent, picks, gain, router, w_query, w_kv, w_out):
    n_dp, n_seq = lax.axis_size("dp"), lax.axis_size("seq")
    n = math.isqrt(n_seq)
    tokens, width = hidden.shape[1:]
    half_heads = w_query.shape[1] // 2
    group_heads = half_heads // HEAD
    out_slab = w_out.shape[0]
    keys = n * SLOTS
    lanes = 2 * group_heads * SLOTS
    vmem = pl.BlockSpec(memory_space=pltpu.VMEM)
    dma = pltpu.SemaphoreType.DMA
    outs = pl.pallas_call(
        functools.partial(kernel, n, n_dp, width, group_heads),
        out_shape=(
            jax.ShapeDtypeStruct(hidden.shape, BF16),
            jax.ShapeDtypeStruct(hidden.shape, BF16),
            jax.ShapeDtypeStruct((SLOTS, 256), F32),
            jax.ShapeDtypeStruct((1, SLOTS), F32),
        ),
        in_specs=[vmem] * 8,
        out_specs=(vmem,) * 4,
        scratch_shapes=[
            pltpu.VMEM((2, n, n, SLOTS, half_heads + 128), BF16),
            pltpu.VMEM((2, n, n, out_slab, width // 2), BF16),
            pltpu.VMEM((n, n, SLOTS, 256), BF16),
            pltpu.VMEM((n, 256, keys), BF16),
            pltpu.VMEM((n, keys, lanes), F32),
            pltpu.VMEM((n, keys, lanes), F32),
            pltpu.VMEM((lanes, 128), BF16),
            pltpu.VMEM((lanes, 128), BF16),
            pltpu.VMEM((n, keys, 256), WIRE),
            pltpu.VMEM((n, keys, 256), WIRE),
            pltpu.VMEM((n, SLOTS, 256), F32),
            pltpu.VMEM((n, SLOTS, 256), F32),
            pltpu.VMEM((n, SLOTS, 256), BF16),
            pltpu.VMEM((n, SLOTS, width), BF16),
            pltpu.VMEM((n, n, SLOTS, keys), BF16),
            pltpu.VMEM((n, SLOTS, 256), F32),
            pltpu.VMEM((n, SLOTS, 256), F32),
            pltpu.VMEM((n_dp, SLOTS, 256), F32),
            pltpu.VMEM((n, 1, width), F32),
            pltpu.VMEM((n, 1, width), F32),
            pltpu.VMEM((n_dp, 1, width), F32),
            pltpu.VMEM((SLOTS, width), F32),
            pltpu.VMEM((SLOTS, width), BF16),
            pltpu.VMEM((SLOTS, width), BF16),
            pltpu.VMEM((2, SLOTS, half_heads + 128), BF16),
            pltpu.VMEM((SLOTS, width), F32),
            dma((2, n)),
            dma((2, n)),
            dma((2, n // 2, 2)),
            dma((2, n // 2, 2)),
            dma((2, n)),
            dma((2, n)),
            dma((5, n)),
            dma((5, n)),
            dma((4, n)),
            dma((4, n)),
            dma((2, n_dp)),
            dma((2, n_dp)),
        ],
        compiler_params=pltpu.CompilerParams(
            collective_id=0, has_side_effects=True, vmem_limit_bytes=58 * 1024 * 1024
        ),
    )(
        hidden, cotangent, picks, gain.reshape(1, -1), router.reshape(1, -1), w_query, w_kv, w_out
    )
    mixed, input_grad, kv_grad, router_grad = outs
    return mixed, input_grad, kv_grad, router_grad.reshape(-1)


def solution(mesh):
    rows = P("dp", "seq", None)
    weight = P("seq", None)
    return jax.shard_map(
        local,
        mesh=mesh,
        in_specs=(rows, rows, P("dp", "seq"), P(), P(), weight, weight, weight),
        out_specs=(rows, rows, weight, P("seq")),
        check_vma=False,
    )
```

time: 808 us -> 143 us (0.18)
  waiting for transfers between devices: 421 us -> 0 us
  blocking collectives: 208 us -> 0 us
  Pallas kernels: 0 us -> 138 us
  local copies, waits for them, and re-layouts: 49.1 us -> 3.91 us
  loops' own time: 43.5 us -> 0 us
  starting transfers between devices: 30.7 us -> 0 us
  matrix products: 26.7 us -> 0 us
  between operations: 14.8 us -> 0.65 us
  other arithmetic: 9.89 us -> 0 us
    unnamed x6 -> x0, waiting for transfers between devices: 242 us -> none
    unnamed x2 -> x0, blocking collectives: 145 us -> none
    pallas_call x0 -> x1, Pallas kernels: none -> 138 us  [local(): pl.pallas_call(functools.partial(kernel, n, n_dp, width, group_heads), ou...]
    reduce_scatter x1 -> x0, waiting for transfers between devices: 89.7 us -> none  [local(): lax.psum_scatter(kv_part, 'seq', scatter_dimension=0, tiled=True)]
    all_gather x3 -> x0, waiting for transfers between devices: 54 us -> none  [the longest x1 54 us: local(): lax.all_gather(w_query, 'seq', axis=0, tiled=True)]
    another operation x1 -> x0, loops' own time: 43.5 us -> none  [carried_in(): return lax.fori_loop(0, peers, lap, start)]
    all_gather x1 -> x0, blocking collectives: 37.7 us -> none  [local(): every_key_value = lax.all_gather(own_kv, 'seq', axis=0, tiled=True)]
    dynamic_slice x64 -> x0, local copies, waits for them, and re-layouts: 37.5 us -> none  [lap(): new = combine(before, everything[k])]
  transfers between devices with their start and end apart: 10 -> 0, of which waited for: 7 -> 0; matrix products, arithmetic and copies ran while one was open for 9% -> 0% of each run, Pallas kernels for 0% -> 0%
where the time goes in v1:
time: 143 us
  Pallas kernels  138 us (97%)
  local copies, waits for them, and re-layouts  3.91 us (3%)
    pallas_call x1, Pallas kernels, local(): pl.pallas_call(functools.partial(kernel, n, n_dp, width, group_heads), ou...  138 us
    unnamed x10, local copies, waits for them, and re-layouts  3.91 us

profile of v1, /device:TPU:1, one launch (start us, length us, event | category | flops | bytes accessed | tf_op | source)
XLA Modules:
  0.0 142.9 jit_solution(8008996481440303764)
XLA Ops:
  0.6 138.3 %shard_map.111 = (bf16[1,128,2048]{2,1,0:T(8,128)(2,1)}, bf16[1,128,2048]{2,1,0:T(8,128)(2,1)}, f32[32,256]{1,0:T(8,128)}, f32[1,32]{1,0:T(1,128)}) custom-call(bf16[1,128,2048]{2,1,0:T(8,128)(2,1)} %hid.1, bf16[1,128,2048]{2,1,0:T(8,128)(2,1)} %cot.1, s32[1,128]{1,0:T(1,128)} %picks.1, f32[1,2048]{1,0:T(1,128)} %bitcast.3, f32[1,2048]{1,0:T(1,128)} %bitcast.4, ...), custom_call_target="tpu_custom_call" | custom-call | tf_op jit(solution)/shard_map/pallas_call | solution.py:523
  138.9 0.0 copy-start
  138.9 1.9 %copy.16 = bf16[1,128,2048]{2,1,0:T(8,128)(2,1)} copy(bf16[1,128,2048]{2,1,0:T(8,128)(2,1)} %get-tuple-element.16) | data formatting | bytes 1048576
  140.9 0.0 copy-done
  140.9 0.0 copy-start.1
  140.9 0.8 copy.17
  141.7 0.0 copy-done.1
  141.7 0.0 copy-start.2
  141.7 0.6 copy.18
  142.3 0.0 copy-done.2
  142.3 0.5 copy.19
Async XLA Ops:
  138.9 2.0 %copy-start = (bf16[1,128,2048]{2,1,0:T(8,128)(2,1)S(1)}, bf16[1,128,2048]{2,1,0:T(8,128)(2,1)}, u32[]{:S(2)}) copy-start(bf16[1,128,2048]{2,1,0:T(8,128)(2,1)} %get-tuple-element.17) | copy-start | bytes 1572868
  140.9 0.8 copy-start.1
  141.7 0.7 copy-start.2

commit v2 on v1

--- a/solution.py
+++ b/solution.py
@@ -17,7 +17,7 @@
 KEY_BOUND = 2.0**64
 NEGATIVE = -1e30
 FAR = 1 << 30
-WIRE = BF16
+PIECES = (4, 2)
 
 
 def dot(left, right, left_dim=1, right_dim=0):
@@ -42,10 +42,10 @@
     hid, cot, picks, gain, router, wq, wkv, wo,
     mixed_out, igrad_out, kvgrad_out, rgrad_out,
     wproj, wout, kv, kvt, scores, dprobs, qpad, opad, dkv, got_dkv, part, got_part,
-    gkv, normed, normed_t, share, got_share, total, row_a, row_b, row_d,
+    gkv, normed, slices, normed_t, share, got_share, total, row_a, row_b, row_d,
     block, block_grad, block_out, dqkv, upstream,
     p1_send, p1_recv, ring_send, ring_recv, sib_send, sib_recv,
-    a_send, a_recv, b_send, b_recv, d_send, d_recv,
+    x_send, x_recv, rs_send, rs_recv, d_send, d_recv,
 ):
     seq, dp = lax.axis_index("seq"), lax.axis_index("dp")
     core = lax.rem(dp, 2)
@@ -67,6 +67,12 @@
     def peer_b(j):
         return (dp, seq_of(lax.rem(b + j, n), a))
 
+    def peer_y(j):
+        return (dp, lax.rem(y + j, n) * n + z)
+
+    def peer_z(j):
+        return (dp, y * n + lax.rem(z + j, n))
+
     def peer_d(j):
         return (lax.rem(dp + j, n_dp), seq)
 
@@ -103,107 +109,6 @@
             wproj[side, y, z, :, :half_heads] = wq[:, cols]
             wproj[side, y, z, :, half_heads:] = wkv[:, side * 128 : (side + 1) * 128]
             wout[side, y, z] = wo[:, side * half_width : (side + 1) * half_width]
-
-    pl.semaphore_wait(barrier, 2 * (n - 1) + n_dp - 1)
-
-    def first(which, ref):
-        def make(j):
-            own = ref.at[core, y, z]
-            return copy_to(own, own, p1_send.at[which, j], p1_recv.at[which, j], peer_a(j))
-
-        return make
-
-    def along_a(which, source, target):
-        def make(j):
-            return copy_to(source(j), target, a_send.at[which, j], a_recv.at[which, j], peer_a(j))
-
-        return make
-
-    def along_b(which, source, target):
-        def make(j):
-            return copy_to(source(j), target, b_send.at[which, j], b_recv.at[which, j], peer_b(j))
-
-        return make
-
-    def along_d(which, ref):
-        def make(j):
-            return copy_to(
-                ref.at[dp], ref.at[dp], d_send.at[which, j], d_recv.at[which, j], peer_d(j)
-            )
-
-        return make
-
-    def start(make, count=n):
-        others(count, lambda j: make(j).start())
-
-    def arrived(make, count=n):
-        others(count, lambda j: make(j).wait_recv())
-
-    def sent(make, count=n):
-        others(count, lambda j: make(j).wait_send())
-
-    last = n // 2 - 1
-
-    def slab(ref, side, k, part_of=None):
-        rows = slice(None) if part_of is None else pl.ds(part_of * (n // 2), n // 2)
-        return ref.at[0, k, rows] if side == 0 else ref.at[1, rows, k]
-
-    def ring_start(which, ref, step):
-        for side in (0, 1):
-
-            @pl.when(core == side)
-            def _():
-                for way, block_id, device in (
-                    (0, lax.rem(b + n - step, n), peer_b(1)),
-                    (1, lax.rem(b + step, n), peer_b(n - 1)),
-                ):
-                    piece = slab(ref, side, block_id, way if step == last else None)
-                    copy_to(
-                        piece,
-                        piece,
-                        ring_send.at[which, step, way],
-                        ring_recv.at[which, step, way],
-                        device,
-                    ).start()
-
-    def ring_copy(which, ref, step, way):
-        piece = slab(ref, 0, 0, way if step == last else None)
-        return copy_to(
-            piece,
-            piece,
-            ring_send.at[which, step, way],
-            ring_recv.at[which, step, way],
-            peer_b(1),
-        )
-
-    def ring_arrived(which, ref, step):
-        for way in (0, 1):
-            ring_copy(which, ref, step, way).wait_recv()
-
-    def sib_start(which, ref, slot, block_id):
-        for side in (0, 1):
-
-            @pl.when(core == side)
-            def _():
-                piece = slab(ref, side, block_id)
-                copy_to(
-                    piece, piece, sib_send.at[which, slot], sib_recv.at[which, slot], sibling
-                ).start()
-
-    def sib_copy(which, ref, slot):
-        piece = slab(ref, 0, 0)
-        return copy_to(piece, piece, sib_send.at[which, slot], sib_recv.at[which, slot], sibling)
-
-    def pass_on(which, ref, step):
-        ring_arrived(which, ref, step)
-        if step < last:
-            ring_start(which, ref, step + 1)
-        sib_start(which, ref, 1 + 2 * step, lax.rem(b + n - 1 - step, n))
-        if step < last:
-            sib_start(which, ref, 2 + 2 * step, lax.rem(b + 1 + step, n))
-
-    start(first(0, wproj))
-    start(first(1, wout))
 
     tokens = hid.shape[1]
     row_id = lax.broadcasted_iota(jnp.int32, (tokens, tokens), 0)
@@ -232,6 +137,120 @@
     logit = lax.fori_loop(0, n_chunks, gate_step, jnp.zeros((tokens, chunk), F32))
     gate = jax.nn.sigmoid(jnp.sum(logit, axis=1, keepdims=True))
 
+    pl.semaphore_wait(barrier, 2 * (n - 1) + n_dp - 1)
+
+    outgoing = []
+
+    def first(which, ref):
+        def make(j):
+            own = ref.at[core, y, z]
+            return copy_to(own, own, p1_send.at[which, j], p1_recv.at[which, j], peer_a(j))
+
+        return make
+
+    def along(peer, which, source, target):
+        def make(j):
+            return copy_to(source(j), target, x_send.at[which, j], x_recv.at[which, j], peer(j))
+
+        return make
+
+    def along_d(which, ref):
+        def make(j):
+            return copy_to(
+                ref.at[dp], ref.at[dp], d_send.at[which, j], d_recv.at[which, j], peer_d(j)
+            )
+
+        return make
+
+    def start(make, count=n):
+        others(count, lambda j: make(j).start())
+        outgoing.append(lambda: sent(make, count))
+
+    def arrived(make, count=n):
+        others(count, lambda j: make(j).wait_recv())
+
+    def sent(make, count=n):
+        others(count, lambda j: make(j).wait_send())
+
+    last = n // 2 - 1
+
+    def slab(ref, side, k, which=0, piece=None):
+        size = n // PIECES[which]
+        rows = slice(None) if piece is None else pl.ds(piece * size, size)
+        return ref.at[0, k, rows] if side == 0 else ref.at[1, rows, k]
+
+    def goes(which, step, way, piece):
+        return step < last or (piece < PIECES[which] // 2) == (way == 0)
+
+    def ring_start(which, ref, step, piece):
+        for side in (0, 1):
+
+            @pl.when(core == side)
+            def _():
+                for way, block_id, device in (
+                    (0, lax.rem(b + n - step, n), peer_b(1)),
+                    (1, lax.rem(b + step, n), peer_b(n - 1)),
+                ):
+                    if goes(which, step, way, piece):
+                        rows = slab(ref, side, block_id, which, piece)
+                        copy_to(
+                            rows,
+                            rows,
+                            ring_send.at[which, step, way, piece],
+                            ring_recv.at[which, step, way, piece],
+                            device,
+                        ).start()
+
+        for way in (0, 1):
+            if goes(which, step, way, piece):
+                outgoing.append(
+                    lambda way=way: ring_copy(which, ref, step, way, piece).wait_send()
+                )
+
+    def ring_copy(which, ref, step, way, piece):
+        rows = slab(ref, 0, 0, which, piece)
+        return copy_to(
+            rows,
+            rows,
+            ring_send.at[which, step, way, piece],
+            ring_recv.at[which, step, way, piece],
+            peer_b(1),
+        )
+
+    def sib_start(which, ref, slot, block_id):
+        for side in (0, 1):
+
+            @pl.when(core == side)
+            def _():
+                rows = slab(ref, side, block_id)
+                copy_to(
+                    rows, rows, sib_send.at[which, slot], sib_recv.at[which, slot], sibling
+                ).start()
+
+        outgoing.append(lambda: sib_copy(which, ref, slot).wait_send())
+
+    def sib_copy(which, ref, slot):
+        rows = slab(ref, 0, 0)
+        return copy_to(rows, rows, sib_send.at[which, slot], sib_recv.at[which, slot], sibling)
+
+    def pass_first(which, ref):
+        for piece in range(PIECES[which]):
+            ring_start(which, ref, 0, piece)
+        sib_start(which, ref, 0, b)
+
+    def pass_on(which, ref, step):
+        for piece in range(PIECES[which]):
+            for way in (0, 1):
+                if goes(which, step, way, piece):
+                    ring_copy(which, ref, step, way, piece).wait_recv()
+            if step < last:
+                ring_start(which, ref, step + 1, piece)
+        sib_start(which, ref, 1 + 2 * step, lax.rem(b + n - 1 - step, n))
+        if step < last:
+            sib_start(which, ref, 2 + 2 * step, lax.rem(b + 1 + step, n))
+
+    start(first(0, wproj))
+
     def pack_step(i, acc):
         rows = dot(pack, hid[0, :, at(i)])
         block[:, at(i)] = rows
@@ -243,24 +262,27 @@
     inv_norm = lax.rsqrt(jnp.sum(squares, axis=1, keepdims=True) * (1.0 / width) + EPSILON)
 
     def norm_step(i):
-        normed[a, :, at(i)] = (block[:, at(i)] * inv_norm * gain[:, at(i)]).astype(BF16)
+        normed[:, at(i)] = (block[:, at(i)] * inv_norm * gain[:, at(i)]).astype(BF16)
 
     each(n_chunks, norm_step)
 
+    slices[y] = normed[:, at(y)]
+    send_slices = along(peer_y, 5, lambda j: normed.at[:, at(lax.rem(y + j, n))], slices.at[y])
+
     arrived(first(0, wproj))
-    ring_start(0, wproj, 0)
-    sib_start(0, wproj, 0, b)
+    pass_first(0, wproj)
+    start(first(1, wout))
+    start(send_slices)
     for step in range(last + 1):
         pass_on(0, wproj, step)
     arrived(first(1, wout))
-    ring_start(1, wout, 0)
-    sib_start(1, wout, 0, b)
+    pass_first(1, wout)
     for slot in range(n):
         sib_copy(0, wproj, slot).wait_recv()
 
     def project(side):
         def step(i, acc):
-            return acc + dot(normed[a, :, at(i)], wproj[side, i].reshape(chunk, -1))
+            return acc + dot(normed[:, at(i)], wproj[side, i].reshape(chunk, -1))
 
         zero = jnp.zeros((SLOTS, half_heads + 128), F32)
         return lax.fori_loop(0, n_chunks, step, zero).astype(BF16)
@@ -298,17 +320,16 @@
     own_keys = jnp.where((lane_id == 0) & (used < 0.5), KEY_MARK, low[:, half_heads:])
     kv[b, a, :, :128] = own_keys.astype(BF16)
     kv[b, a, :, 128:] = high[:, half_heads:].astype(BF16)
-    kv_first = along_a(0, lambda j: kv.at[b, a], kv.at[b, a])
-    kv_second = along_b(0, lambda j: kv.at[b], kv.at[b])
+    kv_first = along(peer_a, 0, lambda j: kv.at[b, a], kv.at[b, a])
+    kv_second = along(peer_b, 1, lambda j: kv.at[b], kv.at[b])
     start(kv_first)
     pad_heads(qpad, low[:, :half_heads], 0)
     pad_heads(qpad, high[:, :half_heads], 1)
     pass_on(1, wout, 0)
     arrived(kv_first)
     start(kv_second)
-    for step in range(1, last):
-        pass_on(1, wout, step)
-    arrived(kv_second)
+    if last > 1:
+        pass_on(1, wout, 1)
 
     key_row = lax.broadcasted_iota(jnp.int32, (keys, 1), 0)
     query_at = seq * SLOTS + (lax.broadcasted_iota(jnp.int32, (1, lanes), 1) & (SLOTS - 1))
@@ -324,19 +345,20 @@
         scores[i] = s
         return jnp.maximum(top, jnp.max(s, axis=0, keepdims=True))
 
-    top = lax.fori_loop(0, n, score_step, jnp.full((1, lanes), NEGATIVE, F32))
-
-    def exp_step(i, acc):
-        e = jnp.exp(scores[i] - top)
-        scores[i] = e
-        return acc + jnp.sum(e, axis=0, keepdims=True)
-
-    inv_sum = 1.0 / lax.fori_loop(0, n, exp_step, jnp.zeros((1, lanes), F32))
+    top = score_step(b, jnp.full((1, lanes), NEGATIVE, F32))
+    for step in range(2, last):
+        pass_on(1, wout, step)
+
+    def next_score_step(t, top):
+        after, odd = lax.div(t, 2), lax.rem(t, 2)
+        j = (1 - odd) * (1 + after) + odd * (n - 1 - after)
+        kv_second(j).wait_recv()
+        return score_step(lax.rem(b + n - j, n), top)
+
+    top = lax.fori_loop(0, n - 1, next_score_step, top)
 
     if last > 0:
         pass_on(1, wout, last)
-    normed_gather = along_a(1, lambda j: normed.at[a], normed.at[a])
-    start(normed_gather)
     for slot in range(n):
         sib_copy(1, wout, slot).wait_recv()
 
@@ -357,41 +379,75 @@
         rows = upstream[:, group * half_heads : (group + 1) * half_heads]
         pad_heads(opad, rows, group)
 
-    def prob_step(i, carry):
-        inner, mixed_t = carry
+    def exp_step(i, carry):
+        total_exp, inner = carry
+        e = jnp.exp(scores[i] - top)
+        scores[i] = e
+        grads = dot(kv[i].reshape(keys, 256)[:, 128:], opad[...], 1, 1)
+        dprobs[i] = grads
+        total_exp += jnp.sum(e, axis=0, keepdims=True)
+        return total_exp, inner + jnp.sum(e * grads, axis=0, keepdims=True)
+
+    zero = jnp.zeros((1, lanes), F32)
+    total_exp, inner = lax.fori_loop(0, n, exp_step, (zero, zero))
+    inv_sum = 1.0 / total_exp
+    inner = inner * inv_sum
+
+    def rs_slab(step, way):
+        return lax.rem(b + n + (1 - 2 * way) * (n // 2 - step), n)
+
+    def rs_copy(step, way, kind):
+        return copy_to(
+            dkv.at[kind, rs_slab(step, way)],
+            got_dkv.at[way, kind, step],
+            rs_send.at[way, kind, step],
+            rs_recv.at[way, kind, step],
+            peer_b(1 + way * (n - 2)),
+        )
+
+    def rs_start(step, way, kind):
+        rs_copy(step, way, kind).start()
+        outgoing.append(lambda: rs_copy(step, way, kind).wait_send())
+
+    def grad_step(t, carry):
+        mixed_t, query_t = carry
+        i = rs_slab(lax.div(t + 1, 2), 1 - lax.rem(t, 2))
         p = scores[i] * inv_sum
-        scores[i] = p
-        dp_ = dot(kv[i].reshape(keys, 256)[:, 128:], opad[...], 1, 1)
-        dprobs[i] = dp_
-        mixed_t += dot(kvt[i, 128:, :], p.astype(BF16))
-        return inner + jnp.sum(p * dp_, axis=0, keepdims=True), mixed_t
-
-    inner, mixed_t = lax.fori_loop(
-        0, n, prob_step, (jnp.zeros((1, lanes), F32), jnp.zeros((128, lanes), F32))
-    )
-
-    send_dkv = along_b(1, lambda j: dkv.at[lax.rem(b + j, n)], got_dkv.at[b])
-
-    def grad_step(j, query_t):
-        i = lax.rem(b + j, n)
-        p = scores[i]
+        half = p.astype(BF16)
         ds = (p * (dprobs[i] - inner)).astype(BF16)
-        dkv[i, :, :128] = (dot(ds, qpad[...]) * scale).astype(WIRE)
-        dkv[i, :, 128:] = dot(p.astype(BF16), opad[...]).astype(WIRE)
-
-        @pl.when(j < n)
+        dkv[0, i] = dot(ds, qpad[...]) * scale
+        dkv[1, i] = dot(half, opad[...])
+
+        @pl.when(t == 0)
         def _():
-            send_dkv(lax.rem(j, n)).start()
-
-        return query_t + dot(kvt[i, :128, :], ds)
-
-    query_t = lax.fori_loop(1, n + 1, grad_step, jnp.zeros((128, lanes), F32))
+            rs_copy(0, 0, 0).start()
+            rs_copy(0, 1, 1).start()
+
+        return mixed_t + dot(kvt[i, 128:, :], half), query_t + dot(kvt[i, :128, :], ds)
+
+    zero = jnp.zeros((128, lanes), F32)
+    mixed_t, query_t = lax.fori_loop(0, n, grad_step, (zero, zero))
+    outgoing.append(lambda: rs_copy(0, 0, 0).wait_send())
+    outgoing.append(lambda: rs_copy(0, 1, 1).wait_send())
+
+    def rs_step(step):
+        for way in (0, 1):
+            for kind in (0, 1):
+                if step > 1 or kind == way:
+                    rs_copy(step - 1, way, kind).wait_recv()
+                    dkv[kind, rs_slab(step, way)] += got_dkv[way, kind, step - 1]
+                rs_start(step, way, kind)
+
+    rs_step(1)
 
     heads = jnp.concatenate(join_heads(mixed_t), axis=1).astype(BF16)
     for side in (0, 1):
         rows = wout[side].reshape(n * out_rows, half_width)
         block_out[:, side * half_width : (side + 1) * half_width] = dot(heads, rows).astype(BF16)
 
+    if last > 1:
+        rs_step(2)
+
     def mix_step(i, acc):
         out_tokens = dot(spread, block_out[:, at(i)])
         mixed_out[0, :, at(i)] = (hid[0, :, at(i)].astype(F32) + gate * out_tokens).astype(BF16)
@@ -406,28 +462,25 @@
         row_a[a, :, at(i)] = jnp.sum(term, axis=0, keepdims=True)
 
     each(n_chunks, router_step)
-    router_first = along_a(2, lambda j: row_a.at[a], row_a.at[a])
-    router_second = along_b(2, lambda j: row_b.at[b], row_b.at[b])
+    router_first = along(peer_a, 2, lambda j: row_a.at[a], row_a.at[a])
+    router_second = along(peer_b, 3, lambda j: row_b.at[b], row_b.at[b])
     router_third = along_d(0, row_d)
     start(router_first)
 
     for group, rows in enumerate(join_heads(query_t * scale)):
         dqkv[group, :, :half_heads] = rows.astype(BF16)
-    arrived(normed_gather)
-
-    def turn_step(i):
-        rows = normed[:, :, at(i)].reshape(keys, chunk).astype(F32)
-        normed_t[i] = jnp.transpose(rows).astype(BF16).reshape(n, SLOTS, keys)
-
-    each(n_chunks, turn_step)
-
-    arrived(send_dkv)
-    mine = dkv[b].astype(F32)
-    mine = lax.fori_loop(
-        1, n, lambda j, acc: acc + got_dkv[lax.rem(b + j, n)].astype(F32), mine
-    )
-    part[...] = mine.reshape(n, SLOTS, 256)
-    send_part = along_a(3, lambda j: part.at[lax.rem(a + j, n)], got_part.at[a])
+    for step in range(3, last + 1):
+        rs_step(step)
+    arrived(send_slices)
+    normed_t[...] = jnp.transpose(slices[...].reshape(keys, chunk).astype(F32)).astype(BF16)
+
+    for kind in (0, 1):
+        mine = dkv[kind, b]
+        for way in (0, 1):
+            rs_copy(last, way, kind).wait_recv()
+            mine += got_dkv[way, kind, last]
+        part[:, :, kind * 128 : (kind + 1) * 128] = mine.reshape(n, SLOTS, 128)
+    send_part = along(peer_a, 4, lambda j: part.at[lax.rem(a + j, n)], got_part.at[a])
     start(send_part)
     arrived(router_first)
     row_b[b] = jnp.sum(row_a[...], axis=0)
@@ -436,8 +489,8 @@
     own = part[a]
     own = lax.fori_loop(1, n, lambda j, acc: acc + got_part[lax.rem(a + j, n)], own)
     grad_kv = own.astype(BF16)
-    gkv[a] = grad_kv
-    gkv_gather = along_a(4, lambda j: gkv.at[a], gkv.at[a])
+    gkv[y] = grad_kv
+    gkv_gather = along(peer_y, 6, lambda j: gkv.at[y], gkv.at[y])
     start(gkv_gather)
     dqkv[0, :, half_heads:] = grad_kv[:, :128]
     dqkv[1, :, half_heads:] = grad_kv[:, 128:]
@@ -449,25 +502,19 @@
         upstream[:, at(i)] = u
         return acc + u * block[:, at(i)]
 
-    along = lax.fori_loop(0, n_chunks, back_step, jnp.zeros((SLOTS, chunk), F32))
-    along = jnp.sum(along, axis=1, keepdims=True) * (1.0 / width)
+    overlap = lax.fori_loop(0, n_chunks, back_step, jnp.zeros((SLOTS, chunk), F32))
+    overlap = jnp.sum(overlap, axis=1, keepdims=True) * (1.0 / width)
 
     arrived(gkv_gather)
-    every = gkv[...].reshape(keys, 256)
-
-    def share_step(i):
-        place = (1 - core) * (i * n + a) + core * (a * n + i)
-        share[i] = dot(normed_t[lax.div(place, n), lax.rem(place, n)], every)
-
-    each(n, share_step)
-    send_share = along_b(3, lambda j: share.at[lax.rem(b + j, n)], got_share.at[b])
+    share[...] = dot(normed_t[...], gkv[...].reshape(keys, 256)).reshape(n, SLOTS, 256)
+    send_share = along(peer_z, 7, lambda j: share.at[lax.rem(z + j, n)], got_share.at[z])
     start(send_share)
 
     arrived(router_second)
     row_d[dp] = jnp.sum(row_b[...], axis=0)
     start(router_third, n_dp)
 
-    cubed = inv_norm * inv_norm * inv_norm * along
+    cubed = inv_norm * inv_norm * inv_norm * overlap
 
     def input_step(i):
         rows = inv_norm * upstream[:, at(i)] - block[:, at(i)] * cubed
@@ -478,8 +525,8 @@
     each(n_chunks, input_step)
 
     arrived(send_share)
-    own = share[b]
-    own = lax.fori_loop(1, n, lambda j, acc: acc + got_share[lax.rem(b + j, n)], own)
+    own = share[z]
+    own = lax.fori_loop(1, n, lambda j, acc: acc + got_share[lax.rem(z + j, n)], own)
     total[dp] = own
     send_total = along_d(1, total)
     start(send_total, n_dp)
@@ -493,20 +540,8 @@
     arrived(send_total, n_dp)
     kvgrad_out[...] = jnp.sum(total[...], axis=0)
 
-    sent(first(0, wproj))
-    sent(first(1, wout))
-    for which, ref in ((0, wproj), (1, wout)):
-        for step in range(last + 1):
-            for way in (0, 1):
-                ring_copy(which, ref, step, way).wait_send()
-        for slot in range(n):
-            sib_copy(which, ref, slot).wait_send()
-    for make in (kv_first, kv_second, normed_gather, send_dkv, router_first, router_second):
-        sent(make)
-    for make in (send_part, gkv_gather, send_share):
-        sent(make)
-    sent(router_third, n_dp)
-    sent(send_total, n_dp)
+    for wait in outgoing:
+        wait()
 
 
 def local(hidden, cotangent, picks, gain, router, w_query, w_kv, w_out):
@@ -539,13 +574,14 @@
             pltpu.VMEM((n, keys, lanes), F32),
             pltpu.VMEM((lanes, 128), BF16),
             pltpu.VMEM((lanes, 128), BF16),
-            pltpu.VMEM((n, keys, 256), WIRE),
-            pltpu.VMEM((n, keys, 256), WIRE),
+            pltpu.VMEM((2, n, keys, 128), F32),
+            pltpu.VMEM((2, 2, n // 2, keys, 128), F32),
             pltpu.VMEM((n, SLOTS, 256), F32),
             pltpu.VMEM((n, SLOTS, 256), F32),
             pltpu.VMEM((n, SLOTS, 256), BF16),
-            pltpu.VMEM((n, SLOTS, width), BF16),
-            pltpu.VMEM((n, n, SLOTS, keys), BF16),
+            pltpu.VMEM((SLOTS, width), BF16),
+            pltpu.VMEM((n, SLOTS, keys), BF16),
+            pltpu.VMEM((keys, keys), BF16),
             pltpu.VMEM((n, SLOTS, 256), F32),
             pltpu.VMEM((n, SLOTS, 256), F32),
             pltpu.VMEM((n_dp, SLOTS, 256), F32),
@@ -559,14 +595,14 @@
             pltpu.VMEM((SLOTS, width), F32),
             dma((2, n)),
             dma((2, n)),
-            dma((2, n // 2, 2)),
-            dma((2, n // 2, 2)),
+            dma((2, n // 2, 2, max(PIECES))),
+            dma((2, n // 2, 2, max(PIECES))),
             dma((2, n)),
             dma((2, n)),
-            dma((5, n)),
-            dma((5, n)),
-            dma((4, n)),
-            dma((4, n)),
+            dma((8, n)),
+            dma((8, n)),
+            dma((2, 2, n // 2)),
+            dma((2, 2, n // 2)),
             dma((2, n_dp)),
             dma((2, n_dp)),
         ],

time: 143 us -> 135 us (0.944)
  Pallas kernels: 138 us -> 130 us
    pallas_call x1, Pallas kernels: 138 us -> 130 us  [local(): pl.pallas_call(functools.partial(kernel, n, n_dp, width, group_heads), ou...]
where the time goes in v2:
time: 135 us
  Pallas kernels  130 us (96%)
  local copies, waits for them, and re-layouts  3.91 us (3%)
    pallas_call x1, Pallas kernels, local(): pl.pallas_call(functools.partial(kernel, n, n_dp, width, group_heads), ou...  130 us
    unnamed x10, local copies, waits for them, and re-layouts  3.91 us

profile of v2, /device:TPU:1, one launch (start us, length us, event | category | flops | bytes accessed | tf_op | source)
XLA Modules:
  0.0 134.5 jit_solution(5369312418985160475)
XLA Ops:
  0.6 129.9 %shard_map.111 = (bf16[1,128,2048]{2,1,0:T(8,128)(2,1)}, bf16[1,128,2048]{2,1,0:T(8,128)(2,1)}, f32[32,256]{1,0:T(8,128)}, f32[1,32]{1,0:T(1,128)}) custom-call(bf16[1,128,2048]{2,1,0:T(8,128)(2,1)} %hid.1, bf16[1,128,2048]{2,1,0:T(8,128)(2,1)} %cot.1, s32[1,128]{1,0:T(1,128)} %picks.1, f32[1,2048]{1,0:T(1,128)} %bitcast.3, f32[1,2048]{1,0:T(1,128)} %bitcast.4, ...), custom_call_target="tpu_custom_call" | custom-call | tf_op jit(solution)/shard_map/pallas_call | solution.py:558
  130.6 0.0 copy-start
  130.6 1.9 %copy.16 = bf16[1,128,2048]{2,1,0:T(8,128)(2,1)} copy(bf16[1,128,2048]{2,1,0:T(8,128)(2,1)} %get-tuple-element.16) | data formatting | bytes 1048576
  132.5 0.0 copy-done
  132.5 0.0 copy-start.1
  132.5 0.8 copy.17
  133.3 0.0 copy-done.1
  133.3 0.0 copy-start.2
  133.3 0.6 copy.18
  133.9 0.0 copy-done.2
  134.0 0.5 copy.19
Async XLA Ops:
  130.6 2.0 %copy-start = (bf16[1,128,2048]{2,1,0:T(8,128)(2,1)S(1)}, bf16[1,128,2048]{2,1,0:T(8,128)(2,1)}, u32[]{:S(2)}) copy-start(bf16[1,128,2048]{2,1,0:T(8,128)(2,1)} %get-tuple-element.17) | copy-start | bytes 1572868
  132.5 0.8 copy-start.1
  133.3 0.7 copy-start.2

commit v3 on v2

--- a/solution.py
+++ b/solution.py
@@ -17,7 +17,7 @@
 KEY_BOUND = 2.0**64
 NEGATIVE = -1e30
 FAR = 1 << 30
-PIECES = (4, 2)
+PIECES = (2, 2)
 
 
 def dot(left, right, left_dim=1, right_dim=0):
@@ -41,7 +41,7 @@
     n, n_dp, width, group_heads,
     hid, cot, picks, gain, router, wq, wkv, wo,
     mixed_out, igrad_out, kvgrad_out, rgrad_out,
-    wproj, wout, kv, kvt, scores, dprobs, qpad, opad, dkv, got_dkv, part, got_part,
+    wquery, wout, wkeys, kv, kvt, scores, dprobs, qpad, opad, dkv, got_dkv, part, got_part,
     gkv, normed, slices, normed_t, share, got_share, total, row_a, row_b, row_d,
     block, block_grad, block_out, dqkv, upstream,
     p1_send, p1_recv, ring_send, ring_recv, sib_send, sib_recv,
@@ -106,8 +106,8 @@
         @pl.when(core == side)
         def _():
             cols = slice(side * half_heads, (side + 1) * half_heads)
-            wproj[side, y, z, :, :half_heads] = wq[:, cols]
-            wproj[side, y, z, :, half_heads:] = wkv[:, side * 128 : (side + 1) * 128]
+            wquery[side, y, z] = wq[:, cols]
+            wkeys[side, y, z] = wkv[:, side * 128 : (side + 1) * 128]
             wout[side, y, z] = wo[:, side * half_width : (side + 1) * half_width]
 
     tokens = hid.shape[1]
@@ -249,7 +249,8 @@
         if step < last:
             sib_start(which, ref, 2 + 2 * step, lax.rem(b + 1 + step, n))
 
-    start(first(0, wproj))
+    start(first(2, wkeys))
+    start(first(0, wquery))
 
     def pack_step(i, acc):
         rows = dot(pack, hid[0, :, at(i)])
@@ -269,23 +270,76 @@
     slices[y] = normed[:, at(y)]
     send_slices = along(peer_y, 5, lambda j: normed.at[:, at(lax.rem(y + j, n))], slices.at[y])
 
-    arrived(first(0, wproj))
-    pass_first(0, wproj)
+    def keys_copy(side, block_id, j):
+        rows = slab(wkeys, side, block_id)
+        return copy_to(rows, rows, x_send.at[8, j], x_recv.at[8, j], peer_b(j))
+
+    def keys_start():
+        for side in (0, 1):
+
+            @pl.when(core == side)
+            def _():
+                others(n, lambda j: keys_copy(side, b, j).start())
+
+        outgoing.append(lambda: others(n, lambda j: keys_copy(0, 0, j).wait_send()))
+
+    def keys_arrived(t):
+        after, odd = lax.div(t, 2), lax.rem(t, 2)
+        j = (1 - odd) * (1 + after) + odd * (n - 1 - after)
+        keys_copy(0, 0, j).wait_recv()
+        for side in (0, 1):
+
+            @pl.when(core == side)
+            def _():
+                rows = slab(wkeys, side, lax.rem(b + n - j, n))
+                copy_to(
+                    rows, rows, sib_send.at[2, t + 1], sib_recv.at[2, t + 1], sibling
+                ).start()
+
+    arrived(first(2, wkeys))
+    keys_start()
+    sib_start(2, wkeys, 0, b)
+    arrived(first(0, wquery))
+    pass_first(0, wquery)
     start(first(1, wout))
-    start(send_slices)
-    for step in range(last + 1):
-        pass_on(0, wproj, step)
+    each(n - 1, keys_arrived)
+    outgoing.append(
+        lambda: others(n, lambda slot: sib_copy(2, wkeys, slot).wait_send())
+    )
+    each(n, lambda slot: sib_copy(2, wkeys, slot).wait_recv())
+
+    def project(ref, side):
+        def step(i, acc):
+            return acc + dot(normed[:, at(i)], ref[side, i].reshape(chunk, -1))
+
+        zero = jnp.zeros((SLOTS, ref.shape[-1]), F32)
+        return lax.fori_loop(0, n_chunks, step, zero).astype(BF16)
+
+    lane_id = lax.broadcasted_iota(jnp.int32, (SLOTS, 128), 1)
+    own_keys = project(wkeys, 0).astype(F32)
+    own_keys = jnp.where((lane_id == 0) & (used < 0.5), KEY_MARK, own_keys)
+    kv[b, a, :, :128] = own_keys.astype(BF16)
+    kv[b, a, :, 128:] = project(wkeys, 1)
+    kv_first = along(peer_a, 0, lambda j: kv.at[b, a], kv.at[b, a])
+    kv_second = along(peer_b, 1, lambda j: kv.at[b], kv.at[b])
+    start(kv_first)
+    pass_on(0, wquery, 0)
     arrived(first(1, wout))
     pass_first(1, wout)
+    arrived(kv_first)
+    start(kv_second)
+    start(send_slices)
+    for which, ref, step in (
+        (0, wquery, 1),
+        (1, wout, 0),
+        (0, wquery, 2),
+        (1, wout, 1),
+        (0, wquery, 3),
+    ):
+        if step <= last:
+            pass_on(which, ref, step)
     for slot in range(n):
-        sib_copy(0, wproj, slot).wait_recv()
-
-    def project(side):
-        def step(i, acc):
-            return acc + dot(normed[:, at(i)], wproj[side, i].reshape(chunk, -1))
-
-        zero = jnp.zeros((SLOTS, half_heads + 128), F32)
-        return lax.fori_loop(0, n_chunks, step, zero).astype(BF16)
+        sib_copy(0, wquery, slot).wait_recv()
 
     low_lane = lax.broadcasted_iota(jnp.int32, (SLOTS, 128), 1) < HEAD
 
@@ -314,22 +368,8 @@
             groups.append(jnp.concatenate(pairs, axis=1))
         return groups
 
-    low = project(0).astype(F32)
-    high = project(1).astype(F32)
-    lane_id = lax.broadcasted_iota(jnp.int32, (SLOTS, 128), 1)
-    own_keys = jnp.where((lane_id == 0) & (used < 0.5), KEY_MARK, low[:, half_heads:])
-    kv[b, a, :, :128] = own_keys.astype(BF16)
-    kv[b, a, :, 128:] = high[:, half_heads:].astype(BF16)
-    kv_first = along(peer_a, 0, lambda j: kv.at[b, a], kv.at[b, a])
-    kv_second = along(peer_b, 1, lambda j: kv.at[b], kv.at[b])
-    start(kv_first)
-    pad_heads(qpad, low[:, :half_heads], 0)
-    pad_heads(qpad, high[:, :half_heads], 1)
-    pass_on(1, wout, 0)
-    arrived(kv_first)
-    start(kv_second)
-    if last > 1:
-        pass_on(1, wout, 1)
+    for group in (0, 1):
+        pad_heads(qpad, project(wquery, group).astype(F32), group)
 
     key_row = lax.broadcasted_iota(jnp.int32, (keys, 1), 0)
     query_at = seq * SLOTS + (lax.broadcasted_iota(jnp.int32, (1, lanes), 1) & (SLOTS - 1))
@@ -346,8 +386,6 @@
         return jnp.maximum(top, jnp.max(s, axis=0, keepdims=True))
 
     top = score_step(b, jnp.full((1, lanes), NEGATIVE, F32))
-    for step in range(2, last):
-        pass_on(1, wout, step)
 
     def next_score_step(t, top):
         after, odd = lax.div(t, 2), lax.rem(t, 2)
@@ -357,8 +395,8 @@
 
     top = lax.fori_loop(0, n - 1, next_score_step, top)
 
-    if last > 0:
-        pass_on(1, wout, last)
+    for step in range(2, last + 1):
+        pass_on(1, wout, step)
     for slot in range(n):
         sib_copy(1, wout, slot).wait_recv()
 
@@ -496,8 +534,10 @@
     dqkv[1, :, half_heads:] = grad_kv[:, 128:]
 
     def back_step(i, acc):
-        grads = dot(dqkv[0], wproj[0, i].reshape(chunk, -1), 1, 1)
-        grads += dot(dqkv[1], wproj[1, i].reshape(chunk, -1), 1, 1)
+        grads = jnp.zeros((SLOTS, chunk), F32)
+        for side in (0, 1):
+            grads += dot(dqkv[side, :, :half_heads], wquery[side, i].reshape(chunk, -1), 1, 1)
+            grads += dot(dqkv[side, :, half_heads:], wkeys[side, i].reshape(chunk, -1), 1, 1)
         u = grads * gain[:, at(i)]
         upstream[:, at(i)] = u
         return acc + u * block[:, at(i)]
@@ -566,8 +606,9 @@
         in_specs=[vmem] * 8,
         out_specs=(vmem,) * 4,
         scratch_shapes=[
-            pltpu.VMEM((2, n, n, SLOTS, half_heads + 128), BF16),
+            pltpu.VMEM((2, n, n, SLOTS, half_heads), BF16),
             pltpu.VMEM((2, n, n, out_slab, width // 2), BF16),
+            pltpu.VMEM((2, n, n, SLOTS, 128), BF16),
             pltpu.VMEM((n, n, SLOTS, 256), BF16),
             pltpu.VMEM((n, 256, keys), BF16),
             pltpu.VMEM((n, keys, lanes), F32),
@@ -593,14 +634,14 @@
             pltpu.VMEM((SLOTS, width), BF16),
             pltpu.VMEM((2, SLOTS, half_heads + 128), BF16),
             pltpu.VMEM((SLOTS, width), F32),
-            dma((2, n)),
-            dma((2, n)),
+            dma((3, n)),
+            dma((3, n)),
             dma((2, n // 2, 2, max(PIECES))),
             dma((2, n // 2, 2, max(PIECES))),
-            dma((2, n)),
-            dma((2, n)),
-            dma((8, n)),
-            dma((8, n)),
+            dma((3, n)),
+            dma((3, n)),
+            dma((9, n)),
+            dma((9, n)),
             dma((2, 2, n // 2)),
             dma((2, 2, n // 2)),
             dma((2, n_dp)),

time: 135 us -> 140 us (1.037)
  Pallas kernels: 130 us -> 135 us
    pallas_call x1, Pallas kernels: 130 us -> 135 us  [local(): pl.pallas_call(functools.partial(kernel, n, n_dp, width, group_heads), ou...]
where the time goes in v3:
time: 140 us
  Pallas kernels  135 us (96%)
  local copies, waits for them, and re-layouts  3.91 us (3%)
    pallas_call x1, Pallas kernels, local(): pl.pallas_call(functools.partial(kernel, n, n_dp, width, group_heads), ou...  135 us
    unnamed x10, local copies, waits for them, and re-layouts  3.91 us

profile of v3, /device:TPU:1, one launch (start us, length us, event | category | flops | bytes accessed | tf_op | source)
XLA Modules:
  0.0 139.5 jit_solution(15597562109791061882)
XLA Ops:
  0.6 135.0 %shard_map.111 = (bf16[1,128,2048]{2,1,0:T(8,128)(2,1)}, bf16[1,128,2048]{2,1,0:T(8,128)(2,1)}, f32[32,256]{1,0:T(8,128)}, f32[1,32]{1,0:T(1,128)}) custom-call(bf16[1,128,2048]{2,1,0:T(8,128)(2,1)} %hid.1, bf16[1,128,2048]{2,1,0:T(8,128)(2,1)} %cot.1, s32[1,128]{1,0:T(1,128)} %picks.1, f32[1,2048]{1,0:T(1,128)} %bitcast.3, f32[1,2048]{1,0:T(1,128)} %bitcast.4, ...), custom_call_target="tpu_custom_call" | custom-call | tf_op jit(solution)/shard_map/pallas_call | solution.py:598
  135.6 0.0 copy-start
  135.6 1.9 %copy.16 = bf16[1,128,2048]{2,1,0:T(8,128)(2,1)} copy(bf16[1,128,2048]{2,1,0:T(8,128)(2,1)} %get-tuple-element.16) | data formatting | bytes 1048576
  137.6 0.0 copy-done
  137.6 0.0 copy-start.1
  137.6 0.8 copy.17
  138.3 0.0 copy-done.1
  138.4 0.0 copy-start.2
  138.4 0.6 copy.18
  139.0 0.0 copy-done.2
  139.0 0.5 copy.19
Async XLA Ops:
  135.6 2.0 %copy-start = (bf16[1,128,2048]{2,1,0:T(8,128)(2,1)S(1)}, bf16[1,128,2048]{2,1,0:T(8,128)(2,1)}, u32[]{:S(2)}) copy-start(bf16[1,128,2048]{2,1,0:T(8,128)(2,1)} %get-tuple-element.17) | copy-start | bytes 1572868
  137.6 0.8 copy-start.1
  138.4 0.7 copy-start.2

commit v4 on v2

--- a/solution.py
+++ b/solution.py
@@ -17,7 +17,7 @@
 KEY_BOUND = 2.0**64
 NEGATIVE = -1e30
 FAR = 1 << 30
-PIECES = (4, 2)
+PIECES = 4
 
 
 def dot(left, right, left_dim=1, right_dim=0):
@@ -42,10 +42,10 @@
     hid, cot, picks, gain, router, wq, wkv, wo,
     mixed_out, igrad_out, kvgrad_out, rgrad_out,
     wproj, wout, kv, kvt, scores, dprobs, qpad, opad, dkv, got_dkv, part, got_part,
-    gkv, normed, slices, normed_t, share, got_share, total, row_a, row_b, row_d,
+    gkv, normed, slices, normed_t, share, pair, got_share, total, final, row_a, row_b, row_d,
     block, block_grad, block_out, dqkv, upstream,
     p1_send, p1_recv, ring_send, ring_recv, sib_send, sib_recv,
-    x_send, x_recv, rs_send, rs_recv, d_send, d_recv,
+    x_send, x_recv, rs_send, rs_recv, d_send, d_recv, o_send, o_recv, t_send, t_recv,
 ):
     seq, dp = lax.axis_index("seq"), lax.axis_index("dp")
     core = lax.rem(dp, 2)
@@ -55,7 +55,8 @@
     keys = n * SLOTS
     half_heads = group_heads * HEAD
     lanes = 2 * group_heads * SLOTS
-    half_width = width // 2
+    chips = n_dp // 2
+    out_cols = width // n_dp
     chunk = keys
 
     def seq_of(b_, a_):
@@ -72,6 +73,9 @@
 
     def peer_z(j):
         return (dp, y * n + lax.rem(z + j, n))
+
+    def peer_x(j):
+        return (lax.rem(dp + 2 * j, n_dp), seq)
 
     def peer_d(j):
         return (lax.rem(dp + j, n_dp), seq)
@@ -108,7 +112,11 @@
             cols = slice(side * half_heads, (side + 1) * half_heads)
             wproj[side, y, z, :, :half_heads] = wq[:, cols]
             wproj[side, y, z, :, half_heads:] = wkv[:, side * 128 : (side + 1) * 128]
-            wout[side, y, z] = wo[:, side * half_width : (side + 1) * half_width]
+
+    def cols_of(d):
+        return pl.ds(pl.multiple_of(d * out_cols, out_cols), out_cols)
+
+    wout[dp, y, z] = wo[:, cols_of(dp)]
 
     tokens = hid.shape[1]
     row_id = lax.broadcasted_iota(jnp.int32, (tokens, tokens), 0)
@@ -141,9 +149,8 @@
 
     outgoing = []
 
-    def first(which, ref):
+    def first(which, own):
         def make(j):
-            own = ref.at[core, y, z]
             return copy_to(own, own, p1_send.at[which, j], p1_recv.at[which, j], peer_a(j))
 
         return make
@@ -174,15 +181,23 @@
 
     last = n // 2 - 1
 
-    def slab(ref, side, k, which=0, piece=None):
-        size = n // PIECES[which]
+    def slab(side, k, piece=None):
+        size = n // PIECES
         rows = slice(None) if piece is None else pl.ds(piece * size, size)
-        return ref.at[0, k, rows] if side == 0 else ref.at[1, rows, k]
-
-    def goes(which, step, way, piece):
-        return step < last or (piece < PIECES[which] // 2) == (way == 0)
-
-    def ring_start(which, ref, step, piece):
+        return wproj.at[0, k, rows] if side == 0 else wproj.at[1, rows, k]
+
+    def goes(step, way, piece):
+        return step < last or (piece < PIECES // 2) == (way == 0)
+
+    def ring_copy(step, way, piece, rows, device):
+        return copy_to(
+            rows, rows, ring_send.at[step, way, piece], ring_recv.at[step, way, piece], device
+        )
+
+    def any_ring_copy(step, way, piece):
+        return ring_copy(step, way, piece, slab(0, 0, piece), peer_b(1))
+
+    def ring_start(step, piece):
         for side in (0, 1):
 
             @pl.when(core == side)
@@ -191,65 +206,85 @@
                     (0, lax.rem(b + n - step, n), peer_b(1)),
                     (1, lax.rem(b + step, n), peer_b(n - 1)),
                 ):
-                    if goes(which, step, way, piece):
-                        rows = slab(ref, side, block_id, which, piece)
-                        copy_to(
-                            rows,
-                            rows,
-                            ring_send.at[which, step, way, piece],
-                            ring_recv.at[which, step, way, piece],
-                            device,
-                        ).start()
+                    if goes(step, way, piece):
+                        ring_copy(step, way, piece, slab(side, block_id, piece), device).start()
 
         for way in (0, 1):
-            if goes(which, step, way, piece):
-                outgoing.append(
-                    lambda way=way: ring_copy(which, ref, step, way, piece).wait_send()
-                )
-
-    def ring_copy(which, ref, step, way, piece):
-        rows = slab(ref, 0, 0, which, piece)
-        return copy_to(
-            rows,
-            rows,
-            ring_send.at[which, step, way, piece],
-            ring_recv.at[which, step, way, piece],
-            peer_b(1),
-        )
-
-    def sib_start(which, ref, slot, block_id):
+            if goes(step, way, piece):
+                outgoing.append(lambda way=way: any_ring_copy(step, way, piece).wait_send())
+
+    def sib_copy(which, slot, rows):
+        return copy_to(rows, rows, sib_send.at[which, slot], sib_recv.at[which, slot], sibling)
+
+    def any_sib_copy(which, slot):
+        return sib_copy(which, slot, slab(0, 0) if which == 0 else wout.at[0])
+
+    def sib_start(slot, block_id):
         for side in (0, 1):
 
             @pl.when(core == side)
             def _():
-                rows = slab(ref, side, block_id)
-                copy_to(
-                    rows, rows, sib_send.at[which, slot], sib_recv.at[which, slot], sibling
-                ).start()
-
-        outgoing.append(lambda: sib_copy(which, ref, slot).wait_send())
-
-    def sib_copy(which, ref, slot):
-        rows = slab(ref, 0, 0)
-        return copy_to(rows, rows, sib_send.at[which, slot], sib_recv.at[which, slot], sibling)
-
-    def pass_first(which, ref):
-        for piece in range(PIECES[which]):
-            ring_start(which, ref, 0, piece)
-        sib_start(which, ref, 0, b)
-
-    def pass_on(which, ref, step):
-        for piece in range(PIECES[which]):
+                sib_copy(0, slot, slab(side, block_id)).start()
+
+        outgoing.append(lambda: any_sib_copy(0, slot).wait_send())
+
+    def pass_on(step):
+        for piece in range(PIECES):
             for way in (0, 1):
-                if goes(which, step, way, piece):
-                    ring_copy(which, ref, step, way, piece).wait_recv()
+                if goes(step, way, piece):
+                    any_ring_copy(step, way, piece).wait_recv()
             if step < last:
-                ring_start(which, ref, step + 1, piece)
-        sib_start(which, ref, 1 + 2 * step, lax.rem(b + n - 1 - step, n))
+                ring_start(step + 1, piece)
+        sib_start(1 + 2 * step, lax.rem(b + n - 1 - step, n))
         if step < last:
-            sib_start(which, ref, 2 + 2 * step, lax.rem(b + 1 + step, n))
-
-    start(first(0, wproj))
+            sib_start(2 + 2 * step, lax.rem(b + 1 + step, n))
+
+    out_first = first(1, wout.at[dp, y, z])
+
+    def out_second(side, j):
+        rows = wout.at[dp, b] if side == 0 else wout.at[dp, :, b]
+        return copy_to(rows, rows, x_send.at[8, j], x_recv.at[8, j], peer_b(j))
+
+    def out_second_start():
+        for side in (0, 1):
+
+            @pl.when(core == side)
+            def _():
+                others(n, lambda j: out_second(side, j).start())
+
+        outgoing.append(lambda: others(n, lambda j: out_second(0, j).wait_send()))
+
+    last_x = chips // 2 - 1
+
+    def out_block(distance):
+        return lax.rem(dp + 2 * n_dp + 2 * distance, n_dp)
+
+    def out_copy(step, way):
+        rows = wout.at[out_block((2 * way - 1) * step)]
+        if step == last_x:
+            rows = rows.at[pl.ds(way * (n // 2), n // 2)]
+        device = peer_x(1 if way == 0 else chips - 1)
+        return copy_to(rows, rows, o_send.at[step, way], o_recv.at[step, way], device)
+
+    def out_start(step):
+        for way in (0, 1):
+            out_copy(step, way).start()
+            outgoing.append(lambda way=way: out_copy(step, way).wait_send())
+
+    def out_sib(slot, distance):
+        sib_copy(1, slot, wout.at[out_block(distance)]).start()
+        outgoing.append(lambda: any_sib_copy(1, slot).wait_send())
+
+    def out_pass_on(step):
+        for way in (0, 1):
+            out_copy(step, way).wait_recv()
+        if step < last_x:
+            out_start(step + 1)
+        out_sib(1 + 2 * step, -1 - step)
+        if step < last_x:
+            out_sib(2 + 2 * step, 1 + step)
+
+    start(first(0, wproj.at[core, y, z]))
 
     def pack_step(i, acc):
         rows = dot(pack, hid[0, :, at(i)])
@@ -269,16 +304,19 @@
     slices[y] = normed[:, at(y)]
     send_slices = along(peer_y, 5, lambda j: normed.at[:, at(lax.rem(y + j, n))], slices.at[y])
 
-    arrived(first(0, wproj))
-    pass_first(0, wproj)
-    start(first(1, wout))
+    arrived(first(0, wproj.at[core, y, z]))
+    for piece in range(PIECES):
+        ring_start(0, piece)
+    sib_start(0, b)
+    start(out_first)
     start(send_slices)
     for step in range(last + 1):
-        pass_on(0, wproj, step)
-    arrived(first(1, wout))
-    pass_first(1, wout)
+        pass_on(step)
+        if step == 0:
+            arrived(out_first)
+            out_second_start()
     for slot in range(n):
-        sib_copy(0, wproj, slot).wait_recv()
+        any_sib_copy(0, slot).wait_recv()
 
     def project(side):
         def step(i, acc):
@@ -325,11 +363,12 @@
     start(kv_first)
     pad_heads(qpad, low[:, :half_heads], 0)
     pad_heads(qpad, high[:, :half_heads], 1)
-    pass_on(1, wout, 0)
+    others(n, lambda j: out_second(0, j).wait_recv())
+    if chips > 1:
+        out_start(0)
+    out_sib(0, 0)
     arrived(kv_first)
     start(kv_second)
-    if last > 1:
-        pass_on(1, wout, 1)
 
     key_row = lax.broadcasted_iota(jnp.int32, (keys, 1), 0)
     query_at = seq * SLOTS + (lax.broadcasted_iota(jnp.int32, (1, lanes), 1) & (SLOTS - 1))
@@ -346,8 +385,8 @@
         return jnp.maximum(top, jnp.max(s, axis=0, keepdims=True))
 
     top = score_step(b, jnp.full((1, lanes), NEGATIVE, F32))
-    for step in range(2, last):
-        pass_on(1, wout, step)
+    for step in range(last_x):
+        out_pass_on(step)
 
     def next_score_step(t, top):
         after, odd = lax.div(t, 2), lax.rem(t, 2)
@@ -357,10 +396,10 @@
 
     top = lax.fori_loop(0, n - 1, next_score_step, top)
 
-    if last > 0:
-        pass_on(1, wout, last)
-    for slot in range(n):
-        sib_copy(1, wout, slot).wait_recv()
+    if chips > 1:
+        out_pass_on(last_x)
+    for slot in range(chips):
+        any_sib_copy(1, slot).wait_recv()
 
     out_rows = n * wout.shape[3]
 
@@ -369,9 +408,8 @@
 
     def head_grad_step(i):
         acc = jnp.zeros((SLOTS, out_rows), F32)
-        for side in (0, 1):
-            part_grad = block_grad[:, side * half_width : (side + 1) * half_width]
-            acc += dot(part_grad, wout[side, i].reshape(out_rows, half_width), 1, 1)
+        for d in range(n_dp):
+            acc += dot(block_grad[:, cols_of(d)], wout[d, i].reshape(out_rows, out_cols), 1, 1)
         upstream[:, out_at(i)] = acc
 
     each(n, head_grad_step)
@@ -441,10 +479,12 @@
     rs_step(1)
 
     heads = jnp.concatenate(join_heads(mixed_t), axis=1).astype(BF16)
-    for side in (0, 1):
-        rows = wout[side].reshape(n * out_rows, half_width)
-        block_out[:, side * half_width : (side + 1) * half_width] = dot(heads, rows).astype(BF16)
-
+
+    def out_step(d):
+        rows = wout[d].reshape(n * out_rows, out_cols)
+        block_out[:, cols_of(d)] = dot(heads, rows).astype(BF16)
+
+    each(n_dp, out_step)
     if last > 1:
         rs_step(2)
 
@@ -507,14 +547,38 @@
 
     arrived(gkv_gather)
     share[...] = dot(normed_t[...], gkv[...].reshape(keys, 256)).reshape(n, SLOTS, 256)
-    send_share = along(peer_z, 7, lambda j: share.at[lax.rem(z + j, n)], got_share.at[z])
-    start(send_share)
-
+    half = n // 2
+    send_pair = copy_to(
+        share.at[pl.ds((1 - core) * half, half)], pair, t_send.at[0], t_recv.at[0], sibling
+    )
+    send_pair.start()
     arrived(router_second)
     row_d[dp] = jnp.sum(row_b[...], axis=0)
     start(router_third, n_dp)
 
     cubed = inv_norm * inv_norm * inv_norm * overlap
+
+    send_pair.wait()
+    for i in range(half):
+        share[core * half + i] += pair[i]
+
+    def share_copy(i):
+        to = core * half + i
+        rows = share.at[to]
+        return copy_to(rows, got_share.at[z], x_send.at[7, i], x_recv.at[7, z], (dp, y * n + to))
+
+    def share_start(i):
+        @pl.when(core * half + i != z)
+        def _():
+            share_copy(i).start()
+
+    def share_sent(i):
+        @pl.when(core * half + i != z)
+        def _():
+            share_copy(i).wait_send()
+
+    each(half, share_start)
+    outgoing.append(lambda: each(half, share_sent))
 
     def input_step(i):
         rows = inv_norm * upstream[:, at(i)] - block[:, at(i)] * cubed
@@ -524,12 +588,27 @@
 
     each(n_chunks, input_step)
 
-    arrived(send_share)
-    own = share[z]
-    own = lax.fori_loop(1, n, lambda j, acc: acc + got_share[lax.rem(z + j, n)], own)
-    total[dp] = own
-    send_total = along_d(1, total)
-    start(send_total, n_dp)
+    def got_share_copy(j):
+        source = lax.rem(z + j, n)
+        return copy_to(
+            share.at[0], got_share.at[source], x_send.at[7, 0], x_recv.at[7, source], sibling
+        )
+
+    x = lax.div(dp, 2)
+
+    def total_copy(j):
+        return copy_to(total.at[x], total.at[x], d_send.at[1, j], d_recv.at[1, j], peer_x(j))
+
+    send_final = copy_to(final, final, t_send.at[1], t_recv.at[1], sibling)
+    here = lax.div(z, half) == core
+
+    @pl.when(here)
+    def _():
+        others(n, lambda j: got_share_copy(j).wait_recv())
+        mine = share[z]
+        total[x] = lax.fori_loop(1, n, lambda j, acc: acc + got_share[lax.rem(z + j, n)], mine)
+        others(chips, lambda j: total_copy(j).start())
+
     arrived(router_third, n_dp)
     row = jnp.sum(row_d[...], axis=0)
     per_tile = 128 // SLOTS
@@ -537,8 +616,20 @@
     for i in range(width // SLOTS):
         tile = jnp.where(seq == i, row[:, i * SLOTS : (i + 1) * SLOTS], tile)
     rgrad_out[...] = tile
-    arrived(send_total, n_dp)
-    kvgrad_out[...] = jnp.sum(total[...], axis=0)
+
+    @pl.when(here)
+    def _():
+        others(chips, lambda j: total_copy(j).wait_recv())
+        final[...] = jnp.sum(total[...], axis=0)
+        send_final.start()
+        others(chips, lambda j: total_copy(j).wait_send())
+        send_final.wait_send()
+
+    @pl.when(jnp.logical_not(here))
+    def _():
+        send_final.wait_recv()
+
+    kvgrad_out[...] = final[...]
 
     for wait in outgoing:
         wait()
@@ -567,7 +658,7 @@
         out_specs=(vmem,) * 4,
         scratch_shapes=[
             pltpu.VMEM((2, n, n, SLOTS, half_heads + 128), BF16),
-            pltpu.VMEM((2, n, n, out_slab, width // 2), BF16),
+            pltpu.VMEM((n_dp, n, n, out_slab, width // n_dp), BF16),
             pltpu.VMEM((n, n, SLOTS, 256), BF16),
             pltpu.VMEM((n, 256, keys), BF16),
             pltpu.VMEM((n, keys, lanes), F32),
@@ -583,8 +674,10 @@
             pltpu.VMEM((n, SLOTS, keys), BF16),
             pltpu.VMEM((keys, keys), BF16),
             pltpu.VMEM((n, SLOTS, 256), F32),
+            pltpu.VMEM((n // 2, SLOTS, 256), F32),
             pltpu.VMEM((n, SLOTS, 256), F32),
-            pltpu.VMEM((n_dp, SLOTS, 256), F32),
+            pltpu.VMEM((n_dp // 2, SLOTS, 256), F32),
+            pltpu.VMEM((SLOTS, 256), F32),
             pltpu.VMEM((n, 1, width), F32),
             pltpu.VMEM((n, 1, width), F32),
             pltpu.VMEM((n_dp, 1, width), F32),
@@ -595,16 +688,20 @@
             pltpu.VMEM((SLOTS, width), F32),
             dma((2, n)),
             dma((2, n)),
-            dma((2, n // 2, 2, max(PIECES))),
-            dma((2, n // 2, 2, max(PIECES))),
-            dma((2, n)),
-            dma((2, n)),
-            dma((8, n)),
-            dma((8, n)),
+            dma((n // 2, 2, PIECES)),
+            dma((n // 2, 2, PIECES)),
+            dma((2, max(n, n_dp // 2))),
+            dma((2, max(n, n_dp // 2))),
+            dma((9, n)),
+            dma((9, n)),
             dma((2, 2, n // 2)),
             dma((2, 2, n // 2)),
             dma((2, n_dp)),
             dma((2, n_dp)),
+            dma((2, 2)),
+            dma((2, 2)),
+            dma((2,)),
+            dma((2,)),
         ],
         compiler_params=pltpu.CompilerParams(
             collective_id=0, has_side_effects=True, vmem_limit_bytes=58 * 1024 * 1024

time: 135 us -> 135 us (level)
  no operation moved by 1% of the time
where the time goes in v4:
time: 135 us
  Pallas kernels  130 us (96%)
  local copies, waits for them, and re-layouts  3.91 us (3%)
    pallas_call x1, Pallas kernels, local(): pl.pallas_call(functools.partial(kernel, n, n_dp, width, group_heads), ou...  130 us
    unnamed x10, local copies, waits for them, and re-layouts  3.91 us

profile of v4, /device:TPU:1, one launch (start us, length us, event | category | flops | bytes accessed | tf_op | source)
XLA Modules:
  0.0 135.1 jit_solution(5435336065495974399)
XLA Ops:
  0.6 130.5 %shard_map.111 = (bf16[1,128,2048]{2,1,0:T(8,128)(2,1)}, bf16[1,128,2048]{2,1,0:T(8,128)(2,1)}, f32[32,256]{1,0:T(8,128)}, f32[1,32]{1,0:T(1,128)}) custom-call(bf16[1,128,2048]{2,1,0:T(8,128)(2,1)} %hid.1, bf16[1,128,2048]{2,1,0:T(8,128)(2,1)} %cot.1, s32[1,128]{1,0:T(1,128)} %picks.1, f32[1,2048]{1,0:T(1,128)} %bitcast.3, f32[1,2048]{1,0:T(1,128)} %bitcast.4, ...), custom_call_target="tpu_custom_call" | custom-call | tf_op jit(solution)/shard_map/pallas_call | solution.py:649
  131.1 0.0 copy-start
  131.1 1.9 %copy.16 = bf16[1,128,2048]{2,1,0:T(8,128)(2,1)} copy(bf16[1,128,2048]{2,1,0:T(8,128)(2,1)} %get-tuple-element.16) | data formatting | bytes 1048576
  133.1 0.0 copy-done
  133.1 0.0 copy-start.1
  133.1 0.8 copy.17
  133.9 0.0 copy-done.1
  133.9 0.0 copy-start.2
  133.9 0.6 copy.18
  134.5 0.0 copy-done.2
  134.5 0.5 copy.19
Async XLA Ops:
  131.1 2.0 %copy-start = (bf16[1,128,2048]{2,1,0:T(8,128)(2,1)S(1)}, bf16[1,128,2048]{2,1,0:T(8,128)(2,1)}, u32[]{:S(2)}) copy-start(bf16[1,128,2048]{2,1,0:T(8,128)(2,1)} %get-tuple-element.17) | copy-start | bytes 1572868
  133.1 0.8 copy-start.1
  133.9 0.7 copy-start.2

commit v5 on v4

--- a/solution.py
+++ b/solution.py
@@ -41,7 +41,7 @@
     n, n_dp, width, group_heads,
     hid, cot, picks, gain, router, wq, wkv, wo,
     mixed_out, igrad_out, kvgrad_out, rgrad_out,
-    wproj, wout, kv, kvt, scores, dprobs, qpad, opad, dkv, got_dkv, part, got_part,
+    wquery, wout, wkeys, kv, kvt, scores, dprobs, qpad, opad, dkv, got_dkv, part, got_part,
     gkv, normed, slices, normed_t, share, pair, got_share, total, final, row_a, row_b, row_d,
     block, block_grad, block_out, dqkv, upstream,
     p1_send, p1_recv, ring_send, ring_recv, sib_send, sib_recv,
@@ -110,8 +110,8 @@
         @pl.when(core == side)
         def _():
             cols = slice(side * half_heads, (side + 1) * half_heads)
-            wproj[side, y, z, :, :half_heads] = wq[:, cols]
-            wproj[side, y, z, :, half_heads:] = wkv[:, side * 128 : (side + 1) * 128]
+            wquery[side, y, z] = wq[:, cols]
+            wkeys[side, y, z] = wkv[:, side * 128 : (side + 1) * 128]
 
     def cols_of(d):
         return pl.ds(pl.multiple_of(d * out_cols, out_cols), out_cols)
@@ -184,7 +184,7 @@
     def slab(side, k, piece=None):
         size = n // PIECES
         rows = slice(None) if piece is None else pl.ds(piece * size, size)
-        return wproj.at[0, k, rows] if side == 0 else wproj.at[1, rows, k]
+        return wquery.at[0, k, rows] if side == 0 else wquery.at[1, rows, k]
 
     def goes(step, way, piece):
         return step < last or (piece < PIECES // 2) == (way == 0)
@@ -217,7 +217,7 @@
         return copy_to(rows, rows, sib_send.at[which, slot], sib_recv.at[which, slot], sibling)
 
     def any_sib_copy(which, slot):
-        return sib_copy(which, slot, slab(0, 0) if which == 0 else wout.at[0])
+        return sib_copy(which, slot, (slab(0, 0), wout.at[0], wkeys.at[0, 0])[which])
 
     def sib_start(slot, block_id):
         for side in (0, 1):
@@ -284,7 +284,10 @@
         if step < last_x:
             out_sib(2 + 2 * step, 1 + step)
 
-    start(first(0, wproj.at[core, y, z]))
+    query_first = first(0, wquery.at[core, y, z])
+    keys_first = first(2, wkeys.at[core, y, z])
+    start(keys_first)
+    start(query_first)
 
     def pack_step(i, acc):
         rows = dot(pack, hid[0, :, at(i)])
@@ -304,26 +307,79 @@
     slices[y] = normed[:, at(y)]
     send_slices = along(peer_y, 5, lambda j: normed.at[:, at(lax.rem(y + j, n))], slices.at[y])
 
-    arrived(first(0, wproj.at[core, y, z]))
+    def keys_slab(side, k):
+        return wkeys.at[0, k] if side == 0 else wkeys.at[1, :, k]
+
+    def keys_copy(side, block_id, j):
+        rows = keys_slab(side, block_id)
+        return copy_to(rows, rows, x_send.at[9, j], x_recv.at[9, j], peer_b(j))
+
+    def nearest(t):
+        after, odd = lax.div(t, 2), lax.rem(t, 2)
+        return (1 - odd) * (1 + after) + odd * (n - 1 - after)
+
+    def keys_sib(slot, block_id):
+        for side in (0, 1):
+
+            @pl.when(core == side)
+            def _():
+                sib_copy(2, slot, keys_slab(side, block_id)).start()
+
+    def keys_arrived(t):
+        j = nearest(t)
+        keys_copy(0, 0, j).wait_recv()
+        keys_sib(t + 1, lax.rem(b + n - j, n))
+
+    arrived(keys_first)
+    for side in (0, 1):
+
+        @pl.when(core == side)
+        def _():
+            others(n, lambda j: keys_copy(side, b, j).start())
+
+    outgoing.append(lambda: others(n, lambda j: keys_copy(0, 0, j).wait_send()))
+    keys_sib(0, b)
+    arrived(query_first)
     for piece in range(PIECES):
         ring_start(0, piece)
     sib_start(0, b)
     start(out_first)
     start(send_slices)
-    for step in range(last + 1):
+    pass_on(0)
+    arrived(out_first)
+    out_second_start()
+    each(n - 1, keys_arrived)
+    outgoing.append(lambda: each(n, lambda slot: any_sib_copy(2, slot).wait_send()))
+    each(n, lambda slot: any_sib_copy(2, slot).wait_recv())
+
+    def project(ref, side):
+        def step(i, acc):
+            return acc + dot(normed[:, at(i)], ref[side, i].reshape(chunk, -1))
+
+        zero = jnp.zeros((SLOTS, ref.shape[-1]), F32)
+        return lax.fori_loop(0, n_chunks, step, zero).astype(BF16)
+
+    lane_id = lax.broadcasted_iota(jnp.int32, (SLOTS, 128), 1)
+    own_keys = project(wkeys, 0).astype(F32)
+    own_keys = jnp.where((lane_id == 0) & (used < 0.5), KEY_MARK, own_keys)
+    kv[b, a, :, :128] = own_keys.astype(BF16)
+    kv[b, a, :, 128:] = project(wkeys, 1)
+    kv_first = along(peer_a, 0, lambda j: kv.at[b, a], kv.at[b, a])
+    kv_second = along(peer_b, 1, lambda j: kv.at[b], kv.at[b])
+    start(kv_first)
+    for step in (1, 2):
+        if step <= last:
+            pass_on(step)
+    arrived(kv_first)
+    start(kv_second)
+    others(n, lambda j: out_second(0, j).wait_recv())
+    if chips > 1:
+        out_start(0)
+    out_sib(0, 0)
+    for step in range(3, last + 1):
         pass_on(step)
-        if step == 0:
-            arrived(out_first)
-            out_second_start()
     for slot in range(n):
         any_sib_copy(0, slot).wait_recv()
-
-    def project(side):
-        def step(i, acc):
-            return acc + dot(normed[:, at(i)], wproj[side, i].reshape(chunk, -1))
-
-        zero = jnp.zeros((SLOTS, half_heads + 128), F32)
-        return lax.fori_loop(0, n_chunks, step, zero).astype(BF16)
 
     low_lane = lax.broadcasted_iota(jnp.int32, (SLOTS, 128), 1) < HEAD
 
@@ -352,23 +408,8 @@
             groups.append(jnp.concatenate(pairs, axis=1))
         return groups
 
-    low = project(0).astype(F32)
-    high = project(1).astype(F32)
-    lane_id = lax.broadcasted_iota(jnp.int32, (SLOTS, 128), 1)
-    own_keys = jnp.where((lane_id == 0) & (used < 0.5), KEY_MARK, low[:, half_heads:])
-    kv[b, a, :, :128] = own_keys.astype(BF16)
-    kv[b, a, :, 128:] = high[:, half_heads:].astype(BF16)
-    kv_first = along(peer_a, 0, lambda j: kv.at[b, a], kv.at[b, a])
-    kv_second = along(peer_b, 1, lambda j: kv.at[b], kv.at[b])
-    start(kv_first)
-    pad_heads(qpad, low[:, :half_heads], 0)
-    pad_heads(qpad, high[:, :half_heads], 1)
-    others(n, lambda j: out_second(0, j).wait_recv())
-    if chips > 1:
-        out_start(0)
-    out_sib(0, 0)
-    arrived(kv_first)
-    start(kv_second)
+    for group in (0, 1):
+        pad_heads(qpad, project(wquery, group).astype(F32), group)
 
     key_row = lax.broadcasted_iota(jnp.int32, (keys, 1), 0)
     query_at = seq * SLOTS + (lax.broadcasted_iota(jnp.int32, (1, lanes), 1) & (SLOTS - 1))
@@ -389,8 +430,7 @@
         out_pass_on(step)
 
     def next_score_step(t, top):
-        after, odd = lax.div(t, 2), lax.rem(t, 2)
-        j = (1 - odd) * (1 + after) + odd * (n - 1 - after)
+        j = nearest(t)
         kv_second(j).wait_recv()
         return score_step(lax.rem(b + n - j, n), top)
 
@@ -536,8 +576,10 @@
     dqkv[1, :, half_heads:] = grad_kv[:, 128:]
 
     def back_step(i, acc):
-        grads = dot(dqkv[0], wproj[0, i].reshape(chunk, -1), 1, 1)
-        grads += dot(dqkv[1], wproj[1, i].reshape(chunk, -1), 1, 1)
+        grads = jnp.zeros((SLOTS, chunk), F32)
+        for side in (0, 1):
+            grads += dot(dqkv[side, :, :half_heads], wquery[side, i].reshape(chunk, -1), 1, 1)
+            grads += dot(dqkv[side, :, half_heads:], wkeys[side, i].reshape(chunk, -1), 1, 1)
         u = grads * gain[:, at(i)]
         upstream[:, at(i)] = u
         return acc + u * block[:, at(i)]
@@ -657,8 +699,9 @@
         in_specs=[vmem] * 8,
         out_specs=(vmem,) * 4,
         scratch_shapes=[
-            pltpu.VMEM((2, n, n, SLOTS, half_heads + 128), BF16),
+            pltpu.VMEM((2, n, n, SLOTS, half_heads), BF16),
             pltpu.VMEM((n_dp, n, n, out_slab, width // n_dp), BF16),
+            pltpu.VMEM((2, n, n, SLOTS, 128), BF16),
             pltpu.VMEM((n, n, SLOTS, 256), BF16),
             pltpu.VMEM((n, 256, keys), BF16),
             pltpu.VMEM((n, keys, lanes), F32),
@@ -686,14 +729,14 @@
             pltpu.VMEM((SLOTS, width), BF16),
             pltpu.VMEM((2, SLOTS, half_heads + 128), BF16),
             pltpu.VMEM((SLOTS, width), F32),
-            dma((2, n)),
-            dma((2, n)),
+            dma((3, n)),
+            dma((3, n)),
             dma((n // 2, 2, PIECES)),
             dma((n // 2, 2, PIECES)),
-            dma((2, max(n, n_dp // 2))),
-            dma((2, max(n, n_dp // 2))),
-            dma((9, n)),
-            dma((9, n)),
+            dma((3, max(n, n_dp // 2))),
+            dma((3, max(n, n_dp // 2))),
+            dma((10, n)),
+            dma((10, n)),
             dma((2, 2, n // 2)),
             dma((2, 2, n // 2)),
             dma((2, n_dp)),

time: 135 us -> 132 us (0.978)
  Pallas kernels: 130 us -> 127 us
    pallas_call x1, Pallas kernels: 130 us -> 127 us  [local(): pl.pallas_call(functools.partial(kernel, n, n_dp, width, group_heads), ou...]
where the time goes in v5:
time: 132 us
  Pallas kernels  127 us (96%)
  local copies, waits for them, and re-layouts  3.91 us (3%)
    pallas_call x1, Pallas kernels, local(): pl.pallas_call(functools.partial(kernel, n, n_dp, width, group_heads), ou...  127 us
    unnamed x10, local copies, waits for them, and re-layouts  3.91 us

profile of v5, /device:TPU:1, one launch (start us, length us, event | category | flops | bytes accessed | tf_op | source)
XLA Modules:
  0.0 131.7 jit_solution(12549546999252923328)
XLA Ops:
  0.6 127.2 %shard_map.111 = (bf16[1,128,2048]{2,1,0:T(8,128)(2,1)}, bf16[1,128,2048]{2,1,0:T(8,128)(2,1)}, f32[32,256]{1,0:T(8,128)}, f32[1,32]{1,0:T(1,128)}) custom-call(bf16[1,128,2048]{2,1,0:T(8,128)(2,1)} %hid.1, bf16[1,128,2048]{2,1,0:T(8,128)(2,1)} %cot.1, s32[1,128]{1,0:T(1,128)} %picks.1, f32[1,2048]{1,0:T(1,128)} %bitcast.3, f32[1,2048]{1,0:T(1,128)} %bitcast.4, ...), custom_call_target="tpu_custom_call" | custom-call | tf_op jit(solution)/shard_map/pallas_call | solution.py:691
  127.8 0.0 copy-start
  127.8 1.9 %copy.16 = bf16[1,128,2048]{2,1,0:T(8,128)(2,1)} copy(bf16[1,128,2048]{2,1,0:T(8,128)(2,1)} %get-tuple-element.16) | data formatting | bytes 1048576
  129.8 0.0 copy-done
  129.8 0.0 copy-start.1
  129.8 0.8 copy.17
  130.6 0.0 copy-done.1
  130.6 0.0 copy-start.2
  130.6 0.6 copy.18
  131.2 0.0 copy-done.2
  131.2 0.5 copy.19
Async XLA Ops:
  127.8 2.0 %copy-start = (bf16[1,128,2048]{2,1,0:T(8,128)(2,1)S(1)}, bf16[1,128,2048]{2,1,0:T(8,128)(2,1)}, u32[]{:S(2)}) copy-start(bf16[1,128,2048]{2,1,0:T(8,128)(2,1)} %get-tuple-element.17) | copy-start | bytes 1572868
  129.8 0.8 copy-start.1
  130.6 0.7 copy-start.2

commit v6 on v5

--- a/solution.py
+++ b/solution.py
@@ -287,6 +287,7 @@
     query_first = first(0, wquery.at[core, y, z])
     keys_first = first(2, wkeys.at[core, y, z])
     start(keys_first)
+    start(out_first)
     start(query_first)
 
     def pack_step(i, acc):
@@ -339,15 +340,12 @@
 
     outgoing.append(lambda: others(n, lambda j: keys_copy(0, 0, j).wait_send()))
     keys_sib(0, b)
+    arrived(out_first)
+    out_second_start()
     arrived(query_first)
     for piece in range(PIECES):
         ring_start(0, piece)
     sib_start(0, b)
-    start(out_first)
-    start(send_slices)
-    pass_on(0)
-    arrived(out_first)
-    out_second_start()
     each(n - 1, keys_arrived)
     outgoing.append(lambda: each(n, lambda slot: any_sib_copy(2, slot).wait_send()))
     each(n, lambda slot: any_sib_copy(2, slot).wait_recv())
@@ -367,17 +365,22 @@
     kv_first = along(peer_a, 0, lambda j: kv.at[b, a], kv.at[b, a])
     kv_second = along(peer_b, 1, lambda j: kv.at[b], kv.at[b])
     start(kv_first)
-    for step in (1, 2):
+    start(send_slices)
+    others(n, lambda j: out_second(0, j).wait_recv())
+    if chips > 1:
+        out_start(0)
+    out_sib(0, 0)
+    for step in (0, 1):
         if step <= last:
             pass_on(step)
     arrived(kv_first)
     start(kv_second)
-    others(n, lambda j: out_second(0, j).wait_recv())
-    if chips > 1:
-        out_start(0)
-    out_sib(0, 0)
-    for step in range(3, last + 1):
+    for step in range(2, last):
         pass_on(step)
+    for step in range(last_x):
+        out_pass_on(step)
+    if last > 1:
+        pass_on(last)
     for slot in range(n):
         any_sib_copy(0, slot).wait_recv()
 
@@ -411,6 +414,27 @@
     for group in (0, 1):
         pad_heads(qpad, project(wquery, group).astype(F32), group)
 
+    if chips > 1:
+        out_pass_on(last_x)
+    for slot in range(chips):
+        any_sib_copy(1, slot).wait_recv()
+
+    out_rows = n * wout.shape[3]
+
+    def out_at(i):
+        return pl.ds(pl.multiple_of(i * out_rows, out_rows), out_rows)
+
+    def head_grad_step(i):
+        acc = jnp.zeros((SLOTS, out_rows), F32)
+        for d in range(n_dp):
+            acc += dot(block_grad[:, cols_of(d)], wout[d, i].reshape(out_rows, out_cols), 1, 1)
+        upstream[:, out_at(i)] = acc
+
+    each(n, head_grad_step)
+    for group in (0, 1):
+        rows = upstream[:, group * half_heads : (group + 1) * half_heads]
+        pad_heads(opad, rows, group)
+
     key_row = lax.broadcasted_iota(jnp.int32, (keys, 1), 0)
     query_at = seq * SLOTS + (lax.broadcasted_iota(jnp.int32, (1, lanes), 1) & (SLOTS - 1))
     scale = HEAD**-0.5
@@ -426,8 +450,6 @@
         return jnp.maximum(top, jnp.max(s, axis=0, keepdims=True))
 
     top = score_step(b, jnp.full((1, lanes), NEGATIVE, F32))
-    for step in range(last_x):
-        out_pass_on(step)
 
     def next_score_step(t, top):
         j = nearest(t)
@@ -435,27 +457,6 @@
         return score_step(lax.rem(b + n - j, n), top)
 
     top = lax.fori_loop(0, n - 1, next_score_step, top)
-
-    if chips > 1:
-        out_pass_on(last_x)
-    for slot in range(chips):
-        any_sib_copy(1, slot).wait_recv()
-
-    out_rows = n * wout.shape[3]
-
-    def out_at(i):
-        return pl.ds(pl.multiple_of(i * out_rows, out_rows), out_rows)
-
-    def head_grad_step(i):
-        acc = jnp.zeros((SLOTS, out_rows), F32)
-        for d in range(n_dp):
-            acc += dot(block_grad[:, cols_of(d)], wout[d, i].reshape(out_rows, out_cols), 1, 1)
-        upstream[:, out_at(i)] = acc
-
-    each(n, head_grad_step)
-    for group in (0, 1):
-        rows = upstream[:, group * half_heads : (group + 1) * half_heads]
-        pad_heads(opad, rows, group)
 
     def exp_step(i, carry):
         total_exp, inner = carry
@@ -474,18 +475,21 @@
     def rs_slab(step, way):
         return lax.rem(b + n + (1 - 2 * way) * (n // 2 - step), n)
 
-    def rs_copy(step, way, kind):
+    half_keys = keys // 2
+
+    def rs_copy(step, way, kind, piece):
+        rows = pl.ds(piece * half_keys, half_keys)
         return copy_to(
-            dkv.at[kind, rs_slab(step, way)],
-            got_dkv.at[way, kind, step],
-            rs_send.at[way, kind, step],
-            rs_recv.at[way, kind, step],
+            dkv.at[kind, rs_slab(step, way), rows],
+            got_dkv.at[way, kind, step, rows],
+            rs_send.at[way, kind, step, piece],
+            rs_recv.at[way, kind, step, piece],
             peer_b(1 + way * (n - 2)),
         )
 
-    def rs_start(step, way, kind):
-        rs_copy(step, way, kind).start()
-        outgoing.append(lambda: rs_copy(step, way, kind).wait_send())
+    def rs_start(step, way, kind, piece):
+        rs_copy(step, way, kind, piece).start()
+        outgoing.append(lambda: rs_copy(step, way, kind, piece).wait_send())
 
     def grad_step(t, carry):
         mixed_t, query_t = carry
@@ -498,23 +502,27 @@
 
         @pl.when(t == 0)
         def _():
-            rs_copy(0, 0, 0).start()
-            rs_copy(0, 1, 1).start()
+            for way in (0, 1):
+                for piece in (0, 1):
+                    rs_copy(0, way, way, piece).start()
 
         return mixed_t + dot(kvt[i, 128:, :], half), query_t + dot(kvt[i, :128, :], ds)
 
     zero = jnp.zeros((128, lanes), F32)
     mixed_t, query_t = lax.fori_loop(0, n, grad_step, (zero, zero))
-    outgoing.append(lambda: rs_copy(0, 0, 0).wait_send())
-    outgoing.append(lambda: rs_copy(0, 1, 1).wait_send())
+    for way in (0, 1):
+        for piece in (0, 1):
+            outgoing.append(
+                lambda way=way, piece=piece: rs_copy(0, way, way, piece).wait_send()
+            )
 
     def rs_step(step):
-        for way in (0, 1):
-            for kind in (0, 1):
-                if step > 1 or kind == way:
-                    rs_copy(step - 1, way, kind).wait_recv()
-                    dkv[kind, rs_slab(step, way)] += got_dkv[way, kind, step - 1]
-                rs_start(step, way, kind)
+        for kind, piece, way in [(k, p, w) for k in (0, 1) for p in (0, 1) for w in (0, 1)]:
+            if step > 1 or kind == way:
+                rs_copy(step - 1, way, kind, piece).wait_recv()
+                rows = slice(piece * half_keys, (piece + 1) * half_keys)
+                dkv[kind, rs_slab(step, way), rows] += got_dkv[way, kind, step - 1, rows]
+            rs_start(step, way, kind, piece)
 
     rs_step(1)
 
@@ -557,7 +565,8 @@
     for kind in (0, 1):
         mine = dkv[kind, b]
         for way in (0, 1):
-            rs_copy(last, way, kind).wait_recv()
+            for piece in (0, 1):
+                rs_copy(last, way, kind, piece).wait_recv()
             mine += got_dkv[way, kind, last]
         part[:, :, kind * 128 : (kind + 1) * 128] = mine.reshape(n, SLOTS, 128)
     send_part = along(peer_a, 4, lambda j: part.at[lax.rem(a + j, n)], got_part.at[a])
@@ -737,8 +746,8 @@
             dma((3, max(n, n_dp // 2))),
             dma((10, n)),
             dma((10, n)),
-            dma((2, 2, n // 2)),
-            dma((2, 2, n // 2)),
+            dma((2, 2, n // 2, 2)),
+            dma((2, 2, n // 2, 2)),
             dma((2, n_dp)),
             dma((2, n_dp)),
             dma((2, 2)),

time: 132 us -> 128 us (0.970)
  Pallas kernels: 127 us -> 123 us
    pallas_call x1, Pallas kernels: 127 us -> 123 us  [local(): pl.pallas_call(functools.partial(kernel, n, n_dp, width, group_heads), ou...]
where the time goes in v6:
time: 128 us
  Pallas kernels  123 us (96%)
  local copies, waits for them, and re-layouts  3.91 us (3%)
    pallas_call x1, Pallas kernels, local(): pl.pallas_call(functools.partial(kernel, n, n_dp, width, group_heads), ou...  123 us
    unnamed x10, local copies, waits for them, and re-layouts  3.91 us

profile of v6, /device:TPU:1, one launch (start us, length us, event | category | flops | bytes accessed | tf_op | source)
XLA Modules:
  0.0 128.0 jit_solution(18334079394364063436)
XLA Ops:
  0.6 123.4 %shard_map.111 = (bf16[1,128,2048]{2,1,0:T(8,128)(2,1)}, bf16[1,128,2048]{2,1,0:T(8,128)(2,1)}, f32[32,256]{1,0:T(8,128)}, f32[1,32]{1,0:T(1,128)}) custom-call(bf16[1,128,2048]{2,1,0:T(8,128)(2,1)} %hid.1, bf16[1,128,2048]{2,1,0:T(8,128)(2,1)} %cot.1, s32[1,128]{1,0:T(1,128)} %picks.1, f32[1,2048]{1,0:T(1,128)} %bitcast.3, f32[1,2048]{1,0:T(1,128)} %bitcast.4, ...), custom_call_target="tpu_custom_call" | custom-call | tf_op jit(solution)/shard_map/pallas_call | solution.py:700
  124.1 0.0 copy-start
  124.1 1.9 %copy.16 = bf16[1,128,2048]{2,1,0:T(8,128)(2,1)} copy(bf16[1,128,2048]{2,1,0:T(8,128)(2,1)} %get-tuple-element.16) | data formatting | bytes 1048576
  126.0 0.0 copy-done
  126.0 0.0 copy-start.1
  126.0 0.8 copy.17
  126.8 0.0 copy-done.1
  126.8 0.0 copy-start.2
  126.8 0.6 copy.18
  127.4 0.0 copy-done.2
  127.5 0.5 copy.19
Async XLA Ops:
  124.1 2.0 %copy-start = (bf16[1,128,2048]{2,1,0:T(8,128)(2,1)S(1)}, bf16[1,128,2048]{2,1,0:T(8,128)(2,1)}, u32[]{:S(2)}) copy-start(bf16[1,128,2048]{2,1,0:T(8,128)(2,1)} %get-tuple-element.17) | copy-start | bytes 1572868
  126.0 0.8 copy-start.1
  126.8 0.7 copy-start.2

commit v7 on v6

--- a/solution.py
+++ b/solution.py
@@ -414,27 +414,6 @@
     for group in (0, 1):
         pad_heads(qpad, project(wquery, group).astype(F32), group)
 
-    if chips > 1:
-        out_pass_on(last_x)
-    for slot in range(chips):
-        any_sib_copy(1, slot).wait_recv()
-
-    out_rows = n * wout.shape[3]
-
-    def out_at(i):
-        return pl.ds(pl.multiple_of(i * out_rows, out_rows), out_rows)
-
-    def head_grad_step(i):
-        acc = jnp.zeros((SLOTS, out_rows), F32)
-        for d in range(n_dp):
-            acc += dot(block_grad[:, cols_of(d)], wout[d, i].reshape(out_rows, out_cols), 1, 1)
-        upstream[:, out_at(i)] = acc
-
-    each(n, head_grad_step)
-    for group in (0, 1):
-        rows = upstream[:, group * half_heads : (group + 1) * half_heads]
-        pad_heads(opad, rows, group)
-
     key_row = lax.broadcasted_iota(jnp.int32, (keys, 1), 0)
     query_at = seq * SLOTS + (lax.broadcasted_iota(jnp.int32, (1, lanes), 1) & (SLOTS - 1))
     scale = HEAD**-0.5
@@ -456,7 +435,29 @@
         kv_second(j).wait_recv()
         return score_step(lax.rem(b + n - j, n), top)
 
-    top = lax.fori_loop(0, n - 1, next_score_step, top)
+    top = lax.fori_loop(0, n // 2, next_score_step, top)
+    if chips > 1:
+        out_pass_on(last_x)
+    for slot in range(chips):
+        any_sib_copy(1, slot).wait_recv()
+
+    out_rows = n * wout.shape[3]
+
+    def out_at(i):
+        return pl.ds(pl.multiple_of(i * out_rows, out_rows), out_rows)
+
+    def head_grad_step(i):
+        acc = jnp.zeros((SLOTS, out_rows), F32)
+        for d in range(n_dp):
+            acc += dot(block_grad[:, cols_of(d)], wout[d, i].reshape(out_rows, out_cols), 1, 1)
+        upstream[:, out_at(i)] = acc
+
+    each(n, head_grad_step)
+    for group in (0, 1):
+        rows = upstream[:, group * half_heads : (group + 1) * half_heads]
+        pad_heads(opad, rows, group)
+
+    top = lax.fori_loop(n // 2, n - 1, next_score_step, top)
 
     def exp_step(i, carry):
         total_exp, inner = carry

time: 128 us -> 128 us (level)
  no operation moved by 1% of the time
where the time goes in v7:
time: 128 us
  Pallas kernels  123 us (96%)
  local copies, waits for them, and re-layouts  3.91 us (3%)
    pallas_call x1, Pallas kernels, local(): pl.pallas_call(functools.partial(kernel, n, n_dp, width, group_heads), ou...  123 us
    unnamed x10, local copies, waits for them, and re-layouts  3.91 us

profile of v7, /device:TPU:1, one launch (start us, length us, event | category | flops | bytes accessed | tf_op | source)
XLA Modules:
  0.0 128.0 jit_solution(15427408620517009142)
XLA Ops:
  0.6 123.5 %shard_map.111 = (bf16[1,128,2048]{2,1,0:T(8,128)(2,1)}, bf16[1,128,2048]{2,1,0:T(8,128)(2,1)}, f32[32,256]{1,0:T(8,128)}, f32[1,32]{1,0:T(1,128)}) custom-call(bf16[1,128,2048]{2,1,0:T(8,128)(2,1)} %hid.1, bf16[1,128,2048]{2,1,0:T(8,128)(2,1)} %cot.1, s32[1,128]{1,0:T(1,128)} %picks.1, f32[1,2048]{1,0:T(1,128)} %bitcast.3, f32[1,2048]{1,0:T(1,128)} %bitcast.4, ...), custom_call_target="tpu_custom_call" | custom-call | tf_op jit(solution)/shard_map/pallas_call | solution.py:701
  124.1 0.0 copy-start
  124.1 1.9 %copy.16 = bf16[1,128,2048]{2,1,0:T(8,128)(2,1)} copy(bf16[1,128,2048]{2,1,0:T(8,128)(2,1)} %get-tuple-element.16) | data formatting | bytes 1048576
  126.1 0.0 copy-done
  126.1 0.0 copy-start.1
  126.1 0.8 copy.17
  126.9 0.0 copy-done.1
  126.9 0.0 copy-start.2
  126.9 0.6 copy.18
  127.5 0.0 copy-done.2
  127.5 0.5 copy.19
Async XLA Ops:
  124.1 2.0 %copy-start = (bf16[1,128,2048]{2,1,0:T(8,128)(2,1)S(1)}, bf16[1,128,2048]{2,1,0:T(8,128)(2,1)}, u32[]{:S(2)}) copy-start(bf16[1,128,2048]{2,1,0:T(8,128)(2,1)} %get-tuple-element.17) | copy-start | bytes 1572868
  126.1 0.8 copy-start.1
  126.9 0.7 copy-start.2
